TPU v7x, 512 devices: a whole 4x8x8 slice. The times are simulated.
512 devices in a mesh: sub: 64 (over x, z_hi, y), shot: 8 (over z_lo, core).
Axes of the slice: x: 4, y: 8, z: 8 (z_hi: 2, z_lo: 4; z = z_hi * 4 + z_lo), core: 2. Of those that a mesh axis runs over, the one named last changes fastest.
Arguments:
- adjoint_source: float32 [8, 2, 64, 16, 8, 256], P('shot', None, 'sub'), may hold values from -6 to 6
- forward_field: float32 [8, 2, 64, 16, 8, 256], P('shot', None, 'sub'), may hold values from -6 to 6
- kappa: float32 [64, 16, 8, 256], P('sub'), may hold values from 1 to 4
- damping: float32 [64, 16, 8, 256], P('sub'), may hold values from 0.1 to 1
Outputs:
- adjoint_field: float32 [8, 2, 64, 16, 8, 256], P('shot', None, 'sub')
- gradient: float32 [64, 16, 8, 256], P('sub', 'shot')
All inputs are finite; a program needn't handle non-finite values.
Results may differ from a plain program's by a relative error of at most 0.00007.
Values sent between devices are 32-bit elements; how exact they have to be, the bound alone decides.
No kernel may reach another device: no remote copies, remote signals or barrier semaphores. Data moves between devices by JAX's collectives and lax.ppermute only.
A program may use at most 64 MiB of HBM per device.

v0:
```python
import jax
import jax.numpy as jnp
from jax import lax
from jax.sharding import PartitionSpec as P

SWEEPS = 4
PX = 4


A_COEF = 2.0 ** (2.0 / 3.0)
B_COEF = 2.0 ** (-4.0 / 3.0)
CENTER = 13.5
RELAX = 0.7


def passed_along(x, axis, by):
    devices = lax.axis_size(axis)
    pairs = [(i, i + by) for i in range(devices) if 0 <= i + by < devices]
    return lax.ppermute(x, axis, pairs)


def through(values, dimension):
    length = values.shape[dimension]
    middle = lax.slice_in_dim(values, 1, length - 1, axis=dimension)
    lower = lax.slice_in_dim(values, 0, length - 2, axis=dimension)
    upper = lax.slice_in_dim(values, 2, length, axis=dimension)
    return A_COEF * middle + B_COEF * (lower + upper)


def padded(values, dimension):
    widths = [(0, 0)] * values.ndim
    widths[dimension] = (1, 1)
    return through(jnp.pad(values, widths), dimension)


def smooth(values):
    for offset in range(3):
        values = padded(values, values.ndim - 3 + offset)
    return values


def cmul(diag_re, diag_im, values):
    real_part = values[:, 0]
    imag_part = values[:, 1]
    return jnp.stack(
        [diag_re * real_part - diag_im * imag_part, diag_re * imag_part + diag_im * real_part],
        axis=1,
    )


def cscale(scale_re, scale_im, values):
    shaped = (-1,) + (1,) * (values.ndim - 2)
    return cmul(scale_re.reshape(shaped), scale_im.reshape(shaped), values)


def inner(left, right):
    dims = tuple(range(1, left.ndim - 1))
    real_part = jnp.sum(left[:, 0] * right[:, 0] + left[:, 1] * right[:, 1], axis=dims)
    imag_part = jnp.sum(left[:, 0] * right[:, 1] - left[:, 1] * right[:, 0], axis=dims)
    return (real_part, imag_part)


def squares(values):
    dims = tuple(range(1, values.ndim - 1))
    return jnp.sum(values[:, 0] * values[:, 0] + values[:, 1] * values[:, 1], axis=dims)


def neighbours_of():
    devices = lax.axis_size("sub")
    across = min(4, devices // 16)
    deepest = devices // (PX * across)
    index = lax.axis_index("sub")
    first = index % PX
    second = index // PX % across
    third = index // (PX * across)
    return [
        (1, first > 0, first < PX - 1),
        (PX, second > 0, second < across - 1),
        (PX * across, third > 0, third < deepest - 1),
    ]


def extend(values, dimension, stride, has_lower, has_upper, depth):
    length = values.shape[dimension]
    top_face = lax.slice_in_dim(values, length - depth, length, axis=dimension)
    bottom_face = lax.slice_in_dim(values, 0, depth, axis=dimension)
    below = passed_along(top_face, "sub", stride)
    above = passed_along(bottom_face, "sub", -stride)
    below = jnp.where(has_lower, below, jnp.zeros_like(below))
    above = jnp.where(has_upper, above, jnp.zeros_like(above))
    return jnp.concatenate([below, values, above], axis=dimension)


def with_rim(values, depth):
    base = values.ndim - 3
    for offset, entry in enumerate(neighbours_of()):
        stride, has_lower, has_upper = entry
        values = extend(values, base + offset, stride, has_lower, has_upper, depth)
    return values


def inner_cells(values):
    return values[..., 1:-1, 1:-1, 1:-1]


def local(adjoint_source, forward_field, kappa, damping):
    local_kappa = kappa[0]
    local_damping = damping[0]
    diag_re = CENTER - local_kappa
    diag_im = local_kappa * local_damping
    pivot_re = diag_re - A_COEF**3
    modulus = pivot_re * pivot_re + diag_im * diag_im
    inv_re = pivot_re / modulus
    inv_im = -diag_im / modulus
    coefficients = jnp.stack([diag_re, diag_im, inv_re, inv_im])
    start = adjoint_source[:, :, 0]

    def sweeps(extended, framed):
        approx = RELAX * cmul(framed[2], framed[3], extended)
        for sweep in range(SWEEPS - 1):
            defect = extended - (cmul(framed[0], framed[1], approx) - smooth(approx))
            approx = approx + RELAX * cmul(framed[2], framed[3], defect)
        return inner_cells(approx)

    def operate(field):
        extended = with_rim(field, 1)
        base = extended.ndim - 3
        neighbours = through(through(through(extended, base), base + 1), base + 2)
        return cmul(diag_re, diag_im, field) - neighbours

    framed = with_rim(coefficients, 1)
    start_ext = with_rim(start, 1)
    first_dir = sweeps(start_ext, framed)
    first_img = operate(first_dir)
    local_re, local_im = inner(first_img, start)
    norm_one, proj_re, proj_im = lax.psum((squares(first_img), local_re, local_im), "sub")
    alpha_re = proj_re / norm_one
    alpha_im = proj_im / norm_one
    solution = cscale(alpha_re, alpha_im, first_dir)
    resid = start - cscale(alpha_re, alpha_im, first_img)
    resid_ext = with_rim(resid, 1)
    second_dir = sweeps(resid_ext, framed)
    second_img = operate(second_dir)
    cross_local_re, cross_local_im = inner(first_img, second_img)
    cross_re, cross_im = lax.psum((cross_local_re, cross_local_im), "sub")
    gamma_re = cross_re / norm_one
    gamma_im = cross_im / norm_one
    new_dir = second_dir - cscale(gamma_re, gamma_im, first_dir)
    new_img = second_img - cscale(gamma_re, gamma_im, first_img)
    pair_re, pair_im = inner(new_img, resid)
    norm_two, next_re, next_im = lax.psum((squares(new_img), pair_re, pair_im), "sub")
    solution = solution + cscale(next_re / norm_two, next_im / norm_two, new_dir)
    wave = forward_field[:, :, 0]
    real_prod = wave[:, 0] * solution[:, 0] + wave[:, 1] * solution[:, 1]
    imag_prod = wave[:, 1] * solution[:, 0] - wave[:, 0] * solution[:, 1]
    partial_terms = jnp.sum(real_prod - local_damping * imag_prod, axis=0)
    summed = lax.psum(partial_terms, "shot")
    rows = summed.shape[0] // lax.axis_size("shot")
    share = lax.dynamic_slice_in_dim(summed, lax.axis_index("shot") * rows, rows, 0)
    return (solution[:, :, None], share[None])


def solution(mesh):
    return jax.shard_map(
        local,
        mesh=mesh,
        in_specs=(
            P("shot", None, "sub", None, None, None),
            P("shot", None, "sub", None, None, None),
            P("sub", None, None, None),
            P("sub", None, None, None),
        ),
        out_specs=(P("shot", None, "sub", None, None, None), P("sub", "shot", None, None)),
        check_vma=False,
    )
```

profile of v0, /device:TPU:1, one launch (start us, length us, event | category | flops | bytes accessed | tf_op | source)
XLA Modules:
  0.0 980.9 jit_solution(7506930683188170077)
XLA Ops:
  9.3 4.7 collective-permute-start.6
  17.2 4.0 collective-permute-start
  22.7 8.2 collective-permute-start.8
  35.0 15.4 %collective-permute-start.2 = (f32[4,18,1,256]{3,2,1,0:T(1,128)S(1)}, f32[4,18,1,256]{3,2,1,0:T(1,128)S(1)}, u32[]{:S(2)}, u32[]{:S(2)}) collective-permute-start(f32[4,18,1,256]{3,2,1,0:T(1,128)S(1)} %get-tuple-element.70), channel_id=1, source_target_pairs={{0,32},{8,40},{16,48},{24,56},{32,64},{40,72},{48,80},{56,88},{64,... | collective-permute-start | bytes 221192 | tf_op jit(solution)/shard_map/ppermute | solution.py:19
  50.4 19.5 %collective-permute-start.10 = (f32[1,2,18,10,1]{4,3,2,1,0:T(8,128)S(1)}, f32[1,2,18,10,1]{4,3,2,1,0:T(8,128)S(1)}, u32[]{:S(2)}, u32[]{:S(2)}) collective-permute-start(f32[1,2,18,10,1]{4,3,2,1,0:T(8,128)S(1)} %get-tuple-element.72), channel_id=1, source_target_pairs={{0,128},{8,136},{16,144},{24,152},{32,160},{40,168},{48,176},{56,1... | collective-permute-start | bytes 4328 | tf_op jit(solution)/shard_map/ppermute | solution.py:19
  69.9 4.4 collective-permute-done.10
  78.6 4.9 collective-permute-start.4
  86.2 2.6 pad_maximum_fusion
  97.3 4.0 collective-permute-start.12
  103.5 17.5 %collective-permute-start.14 = (f32[1,2,18,1,256]{4,3,2,1,0:T(1,128)S(1)}, f32[1,2,18,1,256]{4,3,2,1,0:T(1,128)S(1)}, u32[]{:S(2)}, u32[]{:S(2)}) collective-permute-start(f32[1,2,18,1,256]{4,3,2,1,0:T(1,128)S(1)} %get-tuple-element.80), channel_id=1, source_target_pairs={{0,32},{8,40},{16,48},{24,56},{32,64},{40,72},{48,80},{56,88},{64,... | collective-permute-start | bytes 110600 | tf_op jit(solution)/shard_map/ppermute | solution.py:19
  123.8 20.9 %collective-permute-start.16 = (f32[1,2,18,10,1]{4,3,2,1,0:T(8,128)S(1)}, f32[1,2,18,10,1]{4,3,2,1,0:T(8,128)S(1)}, u32[]{:S(2)}, u32[]{:S(2)}) collective-permute-start(f32[1,2,18,10,1]{4,3,2,1,0:T(8,128)S(1)} %get-tuple-element.68), channel_id=1, source_target_pairs={{0,128},{8,136},{16,144},{24,152},{32,160},{40,168},{48,176},{56,1... | collective-permute-start | bytes 4328 | tf_op jit(solution)/shard_map/ppermute | solution.py:19
  144.7 2.0 collective-permute-done.17
  150.5 191.3 %all-reduce.20 = (f32[1]{0:T(128)}, f32[1]{0:T(128)}, f32[1]{0:T(128)}) all-reduce(f32[1]{0:T(128)} %bitcast.36, f32[1]{0:T(128)} %bitcast.34, f32[1]{0:T(128)} %bitcast.33), channel_id=1, replica_groups=mesh['sub'=64,'shot'=8] {'sub'}, use_global_device_ids=true, to_apply=%region_5.6 | all-reduce | flops 3 | bytes 24 | tf_op jit(solution)/shard_map/psum | solution.py:136
  345.8 4.0 collective-permute-start.18
  352.0 7.9 collective-permute-start.20
  362.6 4.0 collective-permute-start.22
  366.6 2.5 collective-permute-done.23
  379.1 4.3 collective-permute-start.24
  385.6 9.4 collective-permute-start.26
  397.7 17.0 %collective-permute-start.28 = (f32[1,2,18,10,1]{4,3,2,1,0:T(8,128)S(1)}, f32[1,2,18,10,1]{4,3,2,1,0:T(8,128)S(1)}, u32[]{:S(2)}, u32[]{:S(2)}) collective-permute-start(f32[1,2,18,10,1]{4,3,2,1,0:T(8,128)S(1)} %get-tuple-element.64), channel_id=1, source_target_pairs={{0,128},{8,136},{16,144},{24,152},{32,160},{40,168},{48,176},{56,1... | collective-permute-start | bytes 4328 | tf_op jit(solution)/shard_map/ppermute | solution.py:19
  414.8 2.0 collective-permute-done.29
  420.2 189.7 %all-reduce.19 = (f32[1]{0:T(128)}, f32[1]{0:T(128)}) all-reduce(f32[1]{0:T(128)} %bitcast.74, f32[1]{0:T(128)} %bitcast.72), channel_id=1, replica_groups=mesh['sub'=64,'shot'=8] {'sub'}, use_global_device_ids=true, to_apply=%region_9.10 | all-reduce | flops 2 | bytes 16 | tf_op jit(solution)/shard_map/psum | solution.py:145
  614.7 188.0 %all-reduce.18 = (f32[1]{0:T(128)}, f32[1]{0:T(128)}, f32[1]{0:T(128)}) all-reduce(f32[1]{0:T(128)} %bitcast.79, f32[1]{0:T(128)} %bitcast.77, f32[1]{0:T(128)} %bitcast.76), channel_id=1, replica_groups=mesh['sub'=64,'shot'=8] {'sub'}, use_global_device_ids=true, to_apply=%region_15.16 | all-reduce | flops 3 | bytes 24 | tf_op jit(solution)/shard_map/psum | solution.py:151
  808.3 164.4 %all-reduce.23.cloned.1.call-done = f32[16,8,256]{2,1,0:T(8,128)} async-done(((f32[16,8,256]{2,1,0:T(8,128)}), f32[16,8,256]{2,1,0:T(8,128)}) %all-reduce.23.cloned.1.call-update) | async-done | bytes 131088 | tf_op jit(solution)/shard_map/psum | solution.py:157
  (180 shorter events, 65.2 us)
Async XLA Ops:
  7.2 965.5 %all-reduce.23.cloned.1.call-start = ((), (), s32[]{:S(2)}) async-start(), calls=%async_computation | async-start | bytes 262144 | tf_op jit(solution)/shard_map/psum | solution.py:157
  8.0 13.3 %collective-permute-start.7 = (f32[1,2,1,8,256]{4,3,2,1,0:T(8,128)S(1)}, f32[1,2,1,8,256]{4,3,2,1,0:T(8,128)S(1)}, u32[]{:S(2)}, u32[]{:S(2)}) collective-permute-start(f32[1,2,1,8,256]{4,3,2,1,0:T(8,128)S(1)} %get-tuple-element.93), channel_id=1, source_target_pairs={{8,0},{16,8},{24,16},{32,24},{40,32},{48,40},{56,48},{64,56},{72,6... | collective-permute-start | bytes 49160 | tf_op jit(solution)/shard_map/ppermute | solution.py:19
  9.3 12.0 %collective-permute-start.6 = (f32[1,2,1,8,256]{4,3,2,1,0:T(8,128)S(1)}, f32[1,2,1,8,256]{4,3,2,1,0:T(8,128)S(1)}, u32[]{:S(2)}, u32[]{:S(2)}) collective-permute-start(f32[1,2,1,8,256]{4,3,2,1,0:T(8,128)S(1)} %get-tuple-element.92), channel_id=1, source_target_pairs={{0,8},{8,16},{16,24},{24,32},{32,40},{40,48},{48,56},{56,64},{64,7... | collective-permute-start | bytes 49160 | tf_op jit(solution)/shard_map/ppermute | solution.py:19
  15.9 15.0 %collective-permute-start.1 = (f32[4,1,8,256]{3,2,1,0:T(8,128)S(1)}, f32[4,1,8,256]{3,2,1,0:T(8,128)S(1)}, u32[]{:S(2)}, u32[]{:S(2)}) collective-permute-start(f32[4,1,8,256]{3,2,1,0:T(8,128)S(1)} %get-tuple-element.75), channel_id=1, source_target_pairs={{8,0},{16,8},{24,16},{32,24},{40,32},{48,40},{56,48},{64,56},{72,6... | collective-permute-start | bytes 98312 | tf_op jit(solution)/shard_map/ppermute | solution.py:19
  17.2 13.7 %collective-permute-start = (f32[4,1,8,256]{3,2,1,0:T(8,128)S(1)}, f32[4,1,8,256]{3,2,1,0:T(8,128)S(1)}, u32[]{:S(2)}, u32[]{:S(2)}) collective-permute-start(f32[4,1,8,256]{3,2,1,0:T(8,128)S(1)} %get-tuple-element.74), channel_id=1, source_target_pairs={{0,8},{8,16},{16,24},{24,32},{32,40},{40,48},{48,56},{56,64},{64,7... | collective-permute-start | bytes 98312 | tf_op jit(solution)/shard_map/ppermute | solution.py:19
  21.4 9.6 collective-permute-start.9
  22.7 9.3 collective-permute-start.8
  32.3 37.6 %collective-permute-start.11 = (f32[1,2,18,10,1]{4,3,2,1,0:T(8,128)S(1)}, f32[1,2,18,10,1]{4,3,2,1,0:T(8,128)S(1)}, u32[]{:S(2)}, u32[]{:S(2)}) collective-permute-start(f32[1,2,18,10,1]{4,3,2,1,0:T(8,128)S(1)} %get-tuple-element.73), channel_id=1, source_target_pairs={{128,0},{136,8},{144,16},{152,24},{160,32},{168,40},{176,48},{184,... | collective-permute-start | bytes 4328 | tf_op jit(solution)/shard_map/ppermute | solution.py:19
  33.7 40.7 %collective-permute-start.3 = (f32[4,18,1,256]{3,2,1,0:T(1,128)S(1)}, f32[4,18,1,256]{3,2,1,0:T(1,128)S(1)}, u32[]{:S(2)}, u32[]{:S(2)}) collective-permute-start(f32[4,18,1,256]{3,2,1,0:T(1,128)S(1)} %get-tuple-element.71), channel_id=1, source_target_pairs={{32,0},{40,8},{48,16},{56,24},{64,32},{72,40},{80,48},{88,56},{96,... | collective-permute-start | bytes 221192 | tf_op jit(solution)/shard_map/ppermute | solution.py:19
  35.0 39.5 %collective-permute-start.2 = (f32[4,18,1,256]{3,2,1,0:T(1,128)S(1)}, f32[4,18,1,256]{3,2,1,0:T(1,128)S(1)}, u32[]{:S(2)}, u32[]{:S(2)}) collective-permute-start(f32[4,18,1,256]{3,2,1,0:T(1,128)S(1)} %get-tuple-element.70), channel_id=1, source_target_pairs={{0,32},{8,40},{16,48},{24,56},{32,64},{40,72},{48,80},{56,88},{64,... | collective-permute-start | bytes 221192 | tf_op jit(solution)/shard_map/ppermute | solution.py:19
  50.4 24.0 %collective-permute-start.10 = (f32[1,2,18,10,1]{4,3,2,1,0:T(8,128)S(1)}, f32[1,2,18,10,1]{4,3,2,1,0:T(8,128)S(1)}, u32[]{:S(2)}, u32[]{:S(2)}) collective-permute-start(f32[1,2,18,10,1]{4,3,2,1,0:T(8,128)S(1)} %get-tuple-element.72), channel_id=1, source_target_pairs={{0,128},{8,136},{16,144},{24,152},{32,160},{40,168},{48,176},{56,1... | collective-permute-start | bytes 4328 | tf_op jit(solution)/shard_map/ppermute | solution.py:19
  75.3 8.2 collective-permute-start.5
  102.2 18.8 %collective-permute-start.15 = (f32[1,2,18,1,256]{4,3,2,1,0:T(1,128)S(1)}, f32[1,2,18,1,256]{4,3,2,1,0:T(1,128)S(1)}, u32[]{:S(2)}, u32[]{:S(2)}) collective-permute-start(f32[1,2,18,1,256]{4,3,2,1,0:T(1,128)S(1)} %get-tuple-element.81), channel_id=1, source_target_pairs={{32,0},{40,8},{48,16},{56,24},{64,32},{72,40},{80,48},{88,56},{96,... | collective-permute-start | bytes 110600 | tf_op jit(solution)/shard_map/ppermute | solution.py:19
  103.5 18.6 %collective-permute-start.14 = (f32[1,2,18,1,256]{4,3,2,1,0:T(1,128)S(1)}, f32[1,2,18,1,256]{4,3,2,1,0:T(1,128)S(1)}, u32[]{:S(2)}, u32[]{:S(2)}) collective-permute-start(f32[1,2,18,1,256]{4,3,2,1,0:T(1,128)S(1)} %get-tuple-element.80), channel_id=1, source_target_pairs={{0,32},{8,40},{16,48},{24,56},{32,64},{40,72},{48,80},{56,88},{64,... | collective-permute-start | bytes 110600 | tf_op jit(solution)/shard_map/ppermute | solution.py:19
  122.4 24.4 %collective-permute-start.17 = (f32[1,2,18,10,1]{4,3,2,1,0:T(8,128)S(1)}, f32[1,2,18,10,1]{4,3,2,1,0:T(8,128)S(1)}, u32[]{:S(2)}, u32[]{:S(2)}) collective-permute-start(f32[1,2,18,10,1]{4,3,2,1,0:T(8,128)S(1)} %get-tuple-element.69), channel_id=1, source_target_pairs={{128,0},{136,8},{144,16},{152,24},{160,32},{168,40},{176,48},{184,... | collective-permute-start | bytes 4328 | tf_op jit(solution)/shard_map/ppermute | solution.py:19
  123.8 24.8 %collective-permute-start.16 = (f32[1,2,18,10,1]{4,3,2,1,0:T(8,128)S(1)}, f32[1,2,18,10,1]{4,3,2,1,0:T(8,128)S(1)}, u32[]{:S(2)}, u32[]{:S(2)}) collective-permute-start(f32[1,2,18,10,1]{4,3,2,1,0:T(8,128)S(1)} %get-tuple-element.68), channel_id=1, source_target_pairs={{0,128},{8,136},{16,144},{24,152},{32,160},{40,168},{48,176},{56,1... | collective-permute-start | bytes 4328 | tf_op jit(solution)/shard_map/ppermute | solution.py:19
  350.7 9.2 collective-permute-start.21
  352.0 8.9 collective-permute-start.20
  361.3 7.8 collective-permute-start.23
  362.6 7.6 collective-permute-start.22
  384.3 10.7 %collective-permute-start.27 = (f32[1,2,18,1,256]{4,3,2,1,0:T(1,128)S(1)}, f32[1,2,18,1,256]{4,3,2,1,0:T(1,128)S(1)}, u32[]{:S(2)}, u32[]{:S(2)}) collective-permute-start(f32[1,2,18,1,256]{4,3,2,1,0:T(1,128)S(1)} %get-tuple-element.77), channel_id=1, source_target_pairs={{32,0},{40,8},{48,16},{56,24},{64,32},{72,40},{80,48},{88,56},{96,... | collective-permute-start | bytes 110600 | tf_op jit(solution)/shard_map/ppermute | solution.py:19
  385.6 10.4 %collective-permute-start.26 = (f32[1,2,18,1,256]{4,3,2,1,0:T(1,128)S(1)}, f32[1,2,18,1,256]{4,3,2,1,0:T(1,128)S(1)}, u32[]{:S(2)}, u32[]{:S(2)}) collective-permute-start(f32[1,2,18,1,256]{4,3,2,1,0:T(1,128)S(1)} %get-tuple-element.76), channel_id=1, source_target_pairs={{0,32},{8,40},{16,48},{24,56},{32,64},{40,72},{48,80},{56,88},{64,... | collective-permute-start | bytes 110600 | tf_op jit(solution)/shard_map/ppermute | solution.py:19
  396.3 20.5 %collective-permute-start.29 = (f32[1,2,18,10,1]{4,3,2,1,0:T(8,128)S(1)}, f32[1,2,18,10,1]{4,3,2,1,0:T(8,128)S(1)}, u32[]{:S(2)}, u32[]{:S(2)}) collective-permute-start(f32[1,2,18,10,1]{4,3,2,1,0:T(8,128)S(1)} %get-tuple-element.65), channel_id=1, source_target_pairs={{128,0},{136,8},{144,16},{152,24},{160,32},{168,40},{176,48},{184,... | collective-permute-start | bytes 4328 | tf_op jit(solution)/shard_map/ppermute | solution.py:19
  397.7 20.6 %collective-permute-start.28 = (f32[1,2,18,10,1]{4,3,2,1,0:T(8,128)S(1)}, f32[1,2,18,10,1]{4,3,2,1,0:T(8,128)S(1)}, u32[]{:S(2)}, u32[]{:S(2)}) collective-permute-start(f32[1,2,18,10,1]{4,3,2,1,0:T(8,128)S(1)} %get-tuple-element.64), channel_id=1, source_target_pairs={{0,128},{8,136},{16,144},{24,152},{32,160},{40,168},{48,176},{56,1... | collective-permute-start | bytes 4328 | tf_op jit(solution)/shard_map/ppermute | solution.py:19
  (14 other events, 517.4 us)
Sparse Core Ops, SparseCore 0:
  807.7 164.9 all-reduce.22
where the time goes:
time: 984 us; the launch traced here: 981 us
  blocking collectives  569 us (58%)
  waiting for transfers between devices  186 us (19%)
  starting transfers between devices  165 us (17%)
  other arithmetic  30.4 us (3%)
  between operations  23.1 us (2%)
    psum x1, blocking collectives, local(): lax.psum((squares(first_img), local_re, local_im), 'sub')  191 us
    psum x1, blocking collectives, local(): cross_re, cross_im = lax.psum((cross_local_re, cross_local_im), 'sub')  190 us
    psum x1, blocking collectives, local(): lax.psum((squares(new_img), pair_re, pair_im), 'sub')  188 us
    ppermute x30, starting transfers between devices, passed_along(): return lax.ppermute(x, axis, pairs)  165 us
    psum x1, waiting for transfers between devices, local(): summed = lax.psum(partial_terms, 'shot')  164 us
    ppermute x30, waiting for transfers between devices, passed_along(): return lax.ppermute(x, axis, pairs)  21.9 us
  transfers between devices with their start and end apart: 31, of which 15 were waited for; matrix products, arithmetic and copies ran while one was open for 1% of the time, Pallas kernels for 0%

commit v1 on v0

--- a/solution.py
+++ b/solution.py
@@ -129,34 +129,48 @@
         return cmul(diag_re, diag_im, field) - neighbours
 
     framed = with_rim(coefficients, 1)
-    start_ext = with_rim(start, 1)
-    first_dir = sweeps(start_ext, framed)
-    first_img = operate(first_dir)
-    local_re, local_im = inner(first_img, start)
-    norm_one, proj_re, proj_im = lax.psum((squares(first_img), local_re, local_im), "sub")
-    alpha_re = proj_re / norm_one
-    alpha_im = proj_im / norm_one
-    solution = cscale(alpha_re, alpha_im, first_dir)
-    resid = start - cscale(alpha_re, alpha_im, first_img)
-    resid_ext = with_rim(resid, 1)
-    second_dir = sweeps(resid_ext, framed)
+    first_dir = sweeps(with_rim(start, 1), framed)
+    first_wide = with_rim(first_dir, 2)
+    base = first_wide.ndim - 3
+    around = through(through(through(first_wide, base), base + 1), base + 2)
+    first_ext = cmul(framed[0], framed[1], inner_cells(first_wide)) - around
+    first_img = inner_cells(first_ext)
+    second_dir = sweeps(first_ext, framed)
     second_img = operate(second_dir)
-    cross_local_re, cross_local_im = inner(first_img, second_img)
-    cross_re, cross_im = lax.psum((cross_local_re, cross_local_im), "sub")
-    gamma_re = cross_re / norm_one
-    gamma_im = cross_im / norm_one
-    new_dir = second_dir - cscale(gamma_re, gamma_im, first_dir)
-    new_img = second_img - cscale(gamma_re, gamma_im, first_img)
-    pair_re, pair_im = inner(new_img, resid)
-    norm_two, next_re, next_im = lax.psum((squares(new_img), pair_re, pair_im), "sub")
-    solution = solution + cscale(next_re / norm_two, next_im / norm_two, new_dir)
+
+    norm_here = squares(first_img)
+    proj_here = inner(first_img, start)
+    cross_here = inner(first_img, second_img)
+    safe = jnp.where(norm_here > 0, norm_here, 1.0)
+    cross_here = (cross_here[0] / safe, cross_here[1] / safe)
+    part = second_img - cscale(*cross_here, first_img)
+    pair_here = inner(part, start)
+    mine = jnp.stack([norm_here, *proj_here, *cross_here, squares(part), *pair_here])[:, 0]
+    devices = lax.axis_size("sub")
+    table = lax.all_to_all(jnp.broadcast_to(mine[None], (devices, 8)), "sub", 0, 0)
+    norm, proj_re, proj_im, cross_re, cross_im, rest, pair_re, pair_im = [table[:, n] for n in range(8)]
+    total = jnp.sum(norm)
+    alpha_re = jnp.sum(proj_re) / total
+    alpha_im = jnp.sum(proj_im) / total
+    mean_re = jnp.sum(norm * cross_re) / total
+    mean_im = jnp.sum(norm * cross_im) / total
+    off_re = cross_re - mean_re
+    off_im = cross_im - mean_im
+    size = jnp.sum(rest + norm * (off_re * off_re + off_im * off_im))
+    beta_re = jnp.sum(pair_re + off_re * proj_re + off_im * proj_im) / size
+    beta_im = jnp.sum(pair_im + off_re * proj_im - off_im * proj_re) / size
+    lead_re = alpha_re - (beta_re * mean_re - beta_im * mean_im)
+    lead_im = alpha_im - (beta_re * mean_im + beta_im * mean_re)
+    solution = cscale(lead_re, lead_im, first_dir) + cscale(beta_re, beta_im, second_dir)
+
     wave = forward_field[:, :, 0]
     real_prod = wave[:, 0] * solution[:, 0] + wave[:, 1] * solution[:, 1]
     imag_prod = wave[:, 1] * solution[:, 0] - wave[:, 0] * solution[:, 1]
     partial_terms = jnp.sum(real_prod - local_damping * imag_prod, axis=0)
-    summed = lax.psum(partial_terms, "shot")
-    rows = summed.shape[0] // lax.axis_size("shot")
-    share = lax.dynamic_slice_in_dim(summed, lax.axis_index("shot") * rows, rows, 0)
+    shots = lax.axis_size("shot")
+    rows = partial_terms.shape[0] // shots
+    shares = partial_terms.reshape((shots, rows) + partial_terms.shape[1:])
+    share = jnp.sum(lax.all_to_all(shares, "shot", 0, 0), axis=0)
     return (solution[:, :, None], share[None])
 
 

time: 984 us -> 260 us (0.26)
  blocking collectives: 569 us -> 23.1 us
  waiting for transfers between devices: 186 us -> 23.1 us
  between operations: 23.1 us -> 12.2 us
    psum x3 -> x0, blocking collectives: 569 us -> none  [the longest x1 191 us: local(): lax.psum((squares(first_img), local_re, local_im), 'sub')]
    psum x1 -> x0, waiting for transfers between devices: 164 us -> none  [local(): summed = lax.psum(partial_terms, 'shot')]
    all_to_all x0 -> x1, blocking collectives: none -> 23.1 us  [local(): lax.all_to_all(jnp.broadcast_to(mine[None], (devices, 8)), 'sub', 0, 0)]
    ppermute x30 -> x24, starting transfers between devices: 165 us -> 145 us  [passed_along(): return lax.ppermute(x, axis, pairs)]
    all_to_all x0 -> x1, starting transfers between devices: none -> 18.2 us  [local(): share = jnp.sum(lax.all_to_all(shares, 'shot', 0, 0), axis=0)]
    ppermute x30 -> x24, waiting for transfers between devices: 21.9 us -> 18.1 us  [passed_along(): return lax.ppermute(x, axis, pairs)]
  transfers between devices with their start and end apart: 31 -> 25, of which waited for: 15 -> 13; matrix products, arithmetic and copies ran while one was open for 1% -> 2% of each run, Pallas kernels for 0% -> 0%
where the time goes in v1:
time: 260 us; the launch traced here: 259 us
  starting transfers between devices  163 us (63%)
  other arithmetic  29 us (11%)
  waiting for transfers between devices  23.1 us (9%)
  blocking collectives  23.1 us (9%)
  between operations  12.2 us (5%)
  local copies, waits for them, and re-layouts  8.37 us (3%)
    ppermute x24, starting transfers between devices, passed_along(): return lax.ppermute(x, axis, pairs)  145 us
    all_to_all x1, blocking collectives, local(): lax.all_to_all(jnp.broadcast_to(mine[None], (devices, 8)), 'sub', 0, 0)  23.1 us
    all_to_all x1, starting transfers between devices, local(): share = jnp.sum(lax.all_to_all(shares, 'shot', 0, 0), axis=0)  18.2 us
    ppermute x24, waiting for transfers between devices, passed_along(): return lax.ppermute(x, axis, pairs)  18.1 us
    sub x6, other arithmetic, sweeps(): defect = extended - (cmul(framed[0], framed[1], approx) - smooth(approx))  6.33 us
  transfers between devices with their start and end apart: 25, of which 13 were waited for; matrix products, arithmetic and copies ran while one was open for 2% of the time, Pallas kernels for 0%

profile of v1, /device:TPU:1, one launch (start us, length us, event | category | flops | bytes accessed | tf_op | source)
XLA Modules:
  0.0 258.9 jit_solution(3553213104641256734)
XLA Ops:
  2.7 4.7 %collective-permute-start.6 = (f32[1,2,1,8,256]{4,3,2,1,0:T(8,128)S(1)}, f32[1,2,1,8,256]{4,3,2,1,0:T(8,128)S(1)}, u32[]{:S(2)}, u32[]{:S(2)}) collective-permute-start(f32[1,2,1,8,256]{4,3,2,1,0:T(8,128)S(1)} %get-tuple-element.92), channel_id=1, source_target_pairs={{0,8},{8,16},{16,24},{24,32},{32,40},{40,48},{48,56},{56,64},{64,7... | collective-permute-start | bytes 49160 | tf_op jit(solution)/shard_map/ppermute | solution.py:19
  10.7 4.0 %collective-permute-start = (f32[4,1,8,256]{3,2,1,0:T(8,128)S(1)}, f32[4,1,8,256]{3,2,1,0:T(8,128)S(1)}, u32[]{:S(2)}, u32[]{:S(2)}) collective-permute-start(f32[4,1,8,256]{3,2,1,0:T(8,128)S(1)} %get-tuple-element.84), channel_id=1, source_target_pairs={{0,8},{8,16},{16,24},{24,32},{32,40},{40,48},{48,56},{56,64},{64,7... | collective-permute-start | bytes 98312 | tf_op jit(solution)/shard_map/ppermute | solution.py:19
  14.8 1.3 collective-permute-start.9
  16.1 8.2 %collective-permute-start.8 = (f32[1,2,18,1,256]{4,3,2,1,0:T(1,128)S(1)}, f32[1,2,18,1,256]{4,3,2,1,0:T(1,128)S(1)}, u32[]{:S(2)}, u32[]{:S(2)}) collective-permute-start(f32[1,2,18,1,256]{4,3,2,1,0:T(1,128)S(1)} %get-tuple-element.90), channel_id=1, source_target_pairs={{0,32},{8,40},{16,48},{24,56},{32,64},{40,72},{48,80},{56,88},{64,... | collective-permute-start | bytes 110600 | tf_op jit(solution)/shard_map/ppermute | solution.py:19
  28.4 15.4 %collective-permute-start.2 = (f32[4,18,1,256]{3,2,1,0:T(1,128)S(1)}, f32[4,18,1,256]{3,2,1,0:T(1,128)S(1)}, u32[]{:S(2)}, u32[]{:S(2)}) collective-permute-start(f32[4,18,1,256]{3,2,1,0:T(1,128)S(1)} %get-tuple-element.80), channel_id=1, source_target_pairs={{0,32},{8,40},{16,48},{24,56},{32,64},{40,72},{48,80},{56,88},{64,... | collective-permute-start | bytes 221192 | tf_op jit(solution)/shard_map/ppermute | solution.py:19
  43.8 19.5 %collective-permute-start.10 = (f32[1,2,18,10,1]{4,3,2,1,0:T(8,128)S(1)}, f32[1,2,18,10,1]{4,3,2,1,0:T(8,128)S(1)}, u32[]{:S(2)}, u32[]{:S(2)}) collective-permute-start(f32[1,2,18,10,1]{4,3,2,1,0:T(8,128)S(1)} %get-tuple-element.82), channel_id=1, source_target_pairs={{0,128},{8,136},{16,144},{24,152},{32,160},{40,168},{48,176},{56,1... | collective-permute-start | bytes 4328 | tf_op jit(solution)/shard_map/ppermute | solution.py:19
  63.4 4.4 %collective-permute-done.10 = f32[1,2,18,10,1]{4,3,2,1,0:T(8,128)S(1)} collective-permute-done((f32[1,2,18,10,1]{4,3,2,1,0:T(8,128)S(1)}, f32[1,2,18,10,1]{4,3,2,1,0:T(8,128)S(1)}, u32[]{:S(2)}, u32[]{:S(2)}) %collective-permute-start.10) | collective-permute-done | bytes 1472 | tf_op jit(solution)/shard_map/ppermute | solution.py:19
  71.3 4.9 %collective-permute-start.4 = (f32[4,18,10,1]{1,0,3,2:T(4,128)S(1)}, f32[4,18,10,1]{1,0,3,2:T(4,128)S(1)}, u32[]{:S(2)}, u32[]{:S(2)}) collective-permute-start(f32[4,18,10,1]{1,0,3,2:T(4,128)S(1)} %copy.40), channel_id=1, source_target_pairs={{0,128},{8,136},{16,144},{24,152},{32,160},{40,168},{48,176},{56,1... | collective-permute-start | bytes 8648 | tf_op jit(solution)/shard_map/ppermute | solution.py:19
  78.9 2.2 pad_maximum_fusion
  89.6 4.0 %collective-permute-start.12 = (f32[1,2,2,8,256]{4,3,2,1,0:T(8,128)S(1)}, f32[1,2,2,8,256]{4,3,2,1,0:T(8,128)S(1)}, u32[]{:S(2)}, u32[]{:S(2)}) collective-permute-start(f32[1,2,2,8,256]{4,3,2,1,0:T(8,128)S(1)} %get-tuple-element.74), channel_id=1, source_target_pairs={{0,8},{8,16},{16,24},{24,32},{32,40},{40,48},{48,56},{56,64},{64,7... | collective-permute-start | bytes 98312 | tf_op jit(solution)/shard_map/ppermute | solution.py:19
  96.0 17.6 %collective-permute-start.14 = (f32[1,2,20,2,256]{4,3,2,1,0:T(2,128)S(1)}, f32[1,2,20,2,256]{4,3,2,1,0:T(2,128)S(1)}, u32[]{:S(2)}, u32[]{:S(2)}) collective-permute-start(f32[1,2,20,2,256]{4,3,2,1,0:T(2,128)S(1)} %get-tuple-element.86), channel_id=1, source_target_pairs={{0,32},{8,40},{16,48},{24,56},{32,64},{40,72},{48,80},{56,88},{64,... | collective-permute-start | bytes 245768 | tf_op jit(solution)/shard_map/ppermute | solution.py:19
  116.6 21.5 %collective-permute-start.16 = (f32[1,2,20,12,2]{4,3,2,1,0:T(8,128)S(1)}, f32[1,2,20,12,2]{4,3,2,1,0:T(8,128)S(1)}, u32[]{:S(2)}, u32[]{:S(2)}) collective-permute-start(f32[1,2,20,12,2]{4,3,2,1,0:T(8,128)S(1)} %get-tuple-element.76), channel_id=1, source_target_pairs={{0,128},{8,136},{16,144},{24,152},{32,160},{40,168},{48,176},{56,1... | collective-permute-start | bytes 11528 | tf_op jit(solution)/shard_map/ppermute | solution.py:19
  138.2 2.5 collective-permute-done.17
  140.7 2.0 collective-permute-done.16
  152.2 4.0 %collective-permute-start.18 = (f32[1,2,1,8,256]{4,3,2,1,0:T(8,128)S(1)}, f32[1,2,1,8,256]{4,3,2,1,0:T(8,128)S(1)}, u32[]{:S(2)}, u32[]{:S(2)}) collective-permute-start(f32[1,2,1,8,256]{4,3,2,1,0:T(8,128)S(1)} %get-tuple-element.72), channel_id=1, source_target_pairs={{0,8},{8,16},{16,24},{24,32},{32,40},{40,48},{48,56},{56,64},{64,7... | collective-permute-start | bytes 49160 | tf_op jit(solution)/shard_map/ppermute | solution.py:19
  157.1 1.3 collective-permute-start.21
  158.4 8.8 %collective-permute-start.20 = (f32[1,2,18,1,256]{4,3,2,1,0:T(1,128)S(1)}, f32[1,2,18,1,256]{4,3,2,1,0:T(1,128)S(1)}, u32[]{:S(2)}, u32[]{:S(2)}) collective-permute-start(f32[1,2,18,1,256]{4,3,2,1,0:T(1,128)S(1)} %get-tuple-element.88), channel_id=1, source_target_pairs={{0,32},{8,40},{16,48},{24,56},{32,64},{40,72},{48,80},{56,88},{64,... | collective-permute-start | bytes 110600 | tf_op jit(solution)/shard_map/ppermute | solution.py:19
  170.1 16.9 %collective-permute-start.22 = (f32[1,2,18,10,1]{4,3,2,1,0:T(8,128)S(1)}, f32[1,2,18,10,1]{4,3,2,1,0:T(8,128)S(1)}, u32[]{:S(2)}, u32[]{:S(2)}) collective-permute-start(f32[1,2,18,10,1]{4,3,2,1,0:T(8,128)S(1)} %get-tuple-element.78), channel_id=1, source_target_pairs={{0,128},{8,136},{16,144},{24,152},{32,160},{40,168},{48,176},{56,1... | collective-permute-start | bytes 4328 | tf_op jit(solution)/shard_map/ppermute | solution.py:19
  187.0 2.0 collective-permute-done.23
  189.0 1.6 collective-permute-done.22
  196.2 3.8 %stack.263 = f32[8,1]{0,1:T(1,128)S(1)} concatenate(f32[1,1]{0,1:T(1,128)} %bitcast.33, f32[1,1]{0,1:T(1,128)} %bitcast.34, f32[1,1]{0,1:T(1,128)} %bitcast.35, f32[1,1]{0,1:T(1,128)} %bitcast.70, f32[1,1]{0,1:T(1,128)} %bitcast.72, f32[1,1]{0,1:T(1,128)} %bitcast.75, f32[1,1]{0,1:T(1,128)} %bitcast.76, f32[1,1]{0,1:T(1,128)} %bitcast.77), dimensions={0} | concatenate | bytes 64 | tf_op jit(solution)/shard_map/stack | solution.py:148
  200.1 23.1 %all_to_all.14 = f32[64,1,8]{2,1,0:T(1,128)S(1)} all-to-all(f32[64,1,8]{2,1,0:T(1,128)S(1)} %broadcast_in_dim.9), channel_id=1, replica_groups=mesh['sub'=64,'shot'=8] {'sub'}, dimensions={0} | all-to-all | bytes 4096 | tf_op jit(solution)/shard_map/all_to_all | solution.py:150
  234.3 18.2 %all-to-all-start.1 = ((f32[8,2,8,256]{3,2,1,0:T(8,128)}), f32[8,2,8,256]{3,2,1,0:T(8,128)S(1)}, u32[]{:S(2)}, u32[]{:S(2)}) async-start(f32[8,2,8,256]{3,2,1,0:T(8,128)} %bitcast.87), calls=%async_computation.1 | async-start | bytes 262144 | tf_op jit(solution)/shard_map/all_to_all | solution.py:173
  253.2 5.1 %all-to-all-done.1 = f32[8,2,8,256]{3,2,1,0:T(8,128)S(1)} async-done(((f32[8,2,8,256]{3,2,1,0:T(8,128)}), f32[8,2,8,256]{3,2,1,0:T(8,128)S(1)}, u32[]{:S(2)}, u32[]{:S(2)}) %all-to-all-start.1) | async-done | bytes 131104 | tf_op jit(solution)/shard_map/all_to_all | solution.py:173
  (157 shorter events, 49.7 us)
Async XLA Ops:
  1.4 13.3 %collective-permute-start.7 = (f32[1,2,1,8,256]{4,3,2,1,0:T(8,128)S(1)}, f32[1,2,1,8,256]{4,3,2,1,0:T(8,128)S(1)}, u32[]{:S(2)}, u32[]{:S(2)}) collective-permute-start(f32[1,2,1,8,256]{4,3,2,1,0:T(8,128)S(1)} %get-tuple-element.93), channel_id=1, source_target_pairs={{8,0},{16,8},{24,16},{32,24},{40,32},{48,40},{56,48},{64,56},{72,6... | collective-permute-start | bytes 49160 | tf_op jit(solution)/shard_map/ppermute | solution.py:19
  2.7 12.0 %collective-permute-start.6 = (f32[1,2,1,8,256]{4,3,2,1,0:T(8,128)S(1)}, f32[1,2,1,8,256]{4,3,2,1,0:T(8,128)S(1)}, u32[]{:S(2)}, u32[]{:S(2)}) collective-permute-start(f32[1,2,1,8,256]{4,3,2,1,0:T(8,128)S(1)} %get-tuple-element.92), channel_id=1, source_target_pairs={{0,8},{8,16},{16,24},{24,32},{32,40},{40,48},{48,56},{56,64},{64,7... | collective-permute-start | bytes 49160 | tf_op jit(solution)/shard_map/ppermute | solution.py:19
  9.4 15.0 %collective-permute-start.1 = (f32[4,1,8,256]{3,2,1,0:T(8,128)S(1)}, f32[4,1,8,256]{3,2,1,0:T(8,128)S(1)}, u32[]{:S(2)}, u32[]{:S(2)}) collective-permute-start(f32[4,1,8,256]{3,2,1,0:T(8,128)S(1)} %get-tuple-element.85), channel_id=1, source_target_pairs={{8,0},{16,8},{24,16},{32,24},{40,32},{48,40},{56,48},{64,56},{72,6... | collective-permute-start | bytes 98312 | tf_op jit(solution)/shard_map/ppermute | solution.py:19
  10.7 13.8 %collective-permute-start = (f32[4,1,8,256]{3,2,1,0:T(8,128)S(1)}, f32[4,1,8,256]{3,2,1,0:T(8,128)S(1)}, u32[]{:S(2)}, u32[]{:S(2)}) collective-permute-start(f32[4,1,8,256]{3,2,1,0:T(8,128)S(1)} %get-tuple-element.84), channel_id=1, source_target_pairs={{0,8},{8,16},{16,24},{24,32},{32,40},{40,48},{48,56},{56,64},{64,7... | collective-permute-start | bytes 98312 | tf_op jit(solution)/shard_map/ppermute | solution.py:19
  14.8 9.6 %collective-permute-start.9 = (f32[1,2,18,1,256]{4,3,2,1,0:T(1,128)S(1)}, f32[1,2,18,1,256]{4,3,2,1,0:T(1,128)S(1)}, u32[]{:S(2)}, u32[]{:S(2)}) collective-permute-start(f32[1,2,18,1,256]{4,3,2,1,0:T(1,128)S(1)} %get-tuple-element.91), channel_id=1, source_target_pairs={{32,0},{40,8},{48,16},{56,24},{64,32},{72,40},{80,48},{88,56},{96,... | collective-permute-start | bytes 110600 | tf_op jit(solution)/shard_map/ppermute | solution.py:19
  16.1 9.3 %collective-permute-start.8 = (f32[1,2,18,1,256]{4,3,2,1,0:T(1,128)S(1)}, f32[1,2,18,1,256]{4,3,2,1,0:T(1,128)S(1)}, u32[]{:S(2)}, u32[]{:S(2)}) collective-permute-start(f32[1,2,18,1,256]{4,3,2,1,0:T(1,128)S(1)} %get-tuple-element.90), channel_id=1, source_target_pairs={{0,32},{8,40},{16,48},{24,56},{32,64},{40,72},{48,80},{56,88},{64,... | collective-permute-start | bytes 110600 | tf_op jit(solution)/shard_map/ppermute | solution.py:19
  25.7 37.6 %collective-permute-start.11 = (f32[1,2,18,10,1]{4,3,2,1,0:T(8,128)S(1)}, f32[1,2,18,10,1]{4,3,2,1,0:T(8,128)S(1)}, u32[]{:S(2)}, u32[]{:S(2)}) collective-permute-start(f32[1,2,18,10,1]{4,3,2,1,0:T(8,128)S(1)} %get-tuple-element.83), channel_id=1, source_target_pairs={{128,0},{136,8},{144,16},{152,24},{160,32},{168,40},{176,48},{184,... | collective-permute-start | bytes 4328 | tf_op jit(solution)/shard_map/ppermute | solution.py:19
  27.1 40.7 %collective-permute-start.3 = (f32[4,18,1,256]{3,2,1,0:T(1,128)S(1)}, f32[4,18,1,256]{3,2,1,0:T(1,128)S(1)}, u32[]{:S(2)}, u32[]{:S(2)}) collective-permute-start(f32[4,18,1,256]{3,2,1,0:T(1,128)S(1)} %get-tuple-element.81), channel_id=1, source_target_pairs={{32,0},{40,8},{48,16},{56,24},{64,32},{72,40},{80,48},{88,56},{96,... | collective-permute-start | bytes 221192 | tf_op jit(solution)/shard_map/ppermute | solution.py:19
  28.4 39.5 %collective-permute-start.2 = (f32[4,18,1,256]{3,2,1,0:T(1,128)S(1)}, f32[4,18,1,256]{3,2,1,0:T(1,128)S(1)}, u32[]{:S(2)}, u32[]{:S(2)}) collective-permute-start(f32[4,18,1,256]{3,2,1,0:T(1,128)S(1)} %get-tuple-element.80), channel_id=1, source_target_pairs={{0,32},{8,40},{16,48},{24,56},{32,64},{40,72},{48,80},{56,88},{64,... | collective-permute-start | bytes 221192 | tf_op jit(solution)/shard_map/ppermute | solution.py:19
  43.8 24.0 %collective-permute-start.10 = (f32[1,2,18,10,1]{4,3,2,1,0:T(8,128)S(1)}, f32[1,2,18,10,1]{4,3,2,1,0:T(8,128)S(1)}, u32[]{:S(2)}, u32[]{:S(2)}) collective-permute-start(f32[1,2,18,10,1]{4,3,2,1,0:T(8,128)S(1)} %get-tuple-element.82), channel_id=1, source_target_pairs={{0,128},{8,136},{16,144},{24,152},{32,160},{40,168},{48,176},{56,1... | collective-permute-start | bytes 4328 | tf_op jit(solution)/shard_map/ppermute | solution.py:19
  69.0 7.2 %collective-permute-start.5 = (f32[4,18,10,1]{1,0,3,2:T(4,128)S(1)}, f32[4,18,10,1]{1,0,3,2:T(4,128)S(1)}, u32[]{:S(2)}, u32[]{:S(2)}) collective-permute-start(f32[4,18,10,1]{1,0,3,2:T(4,128)S(1)} %copy.41), channel_id=1, source_target_pairs={{128,0},{136,8},{144,16},{152,24},{160,32},{168,40},{176,48},{184,... | collective-permute-start | bytes 8648 | tf_op jit(solution)/shard_map/ppermute | solution.py:19
  71.3 5.8 %collective-permute-start.4 = (f32[4,18,10,1]{1,0,3,2:T(4,128)S(1)}, f32[4,18,10,1]{1,0,3,2:T(4,128)S(1)}, u32[]{:S(2)}, u32[]{:S(2)}) collective-permute-start(f32[4,18,10,1]{1,0,3,2:T(4,128)S(1)} %copy.40), channel_id=1, source_target_pairs={{0,128},{8,136},{16,144},{24,152},{32,160},{40,168},{48,176},{56,1... | collective-permute-start | bytes 8648 | tf_op jit(solution)/shard_map/ppermute | solution.py:19
  88.2 5.4 %collective-permute-start.13 = (f32[1,2,2,8,256]{4,3,2,1,0:T(8,128)S(1)}, f32[1,2,2,8,256]{4,3,2,1,0:T(8,128)S(1)}, u32[]{:S(2)}, u32[]{:S(2)}) collective-permute-start(f32[1,2,2,8,256]{4,3,2,1,0:T(8,128)S(1)} %get-tuple-element.75), channel_id=1, source_target_pairs={{8,0},{16,8},{24,16},{32,24},{40,32},{48,40},{56,48},{64,56},{72,6... | collective-permute-start | bytes 98312 | tf_op jit(solution)/shard_map/ppermute | solution.py:19
  89.6 5.0 %collective-permute-start.12 = (f32[1,2,2,8,256]{4,3,2,1,0:T(8,128)S(1)}, f32[1,2,2,8,256]{4,3,2,1,0:T(8,128)S(1)}, u32[]{:S(2)}, u32[]{:S(2)}) collective-permute-start(f32[1,2,2,8,256]{4,3,2,1,0:T(8,128)S(1)} %get-tuple-element.74), channel_id=1, source_target_pairs={{0,8},{8,16},{16,24},{24,32},{32,40},{40,48},{48,56},{56,64},{64,7... | collective-permute-start | bytes 98312 | tf_op jit(solution)/shard_map/ppermute | solution.py:19
  94.7 19.1 %collective-permute-start.15 = (f32[1,2,20,2,256]{4,3,2,1,0:T(2,128)S(1)}, f32[1,2,20,2,256]{4,3,2,1,0:T(2,128)S(1)}, u32[]{:S(2)}, u32[]{:S(2)}) collective-permute-start(f32[1,2,20,2,256]{4,3,2,1,0:T(2,128)S(1)} %get-tuple-element.87), channel_id=1, source_target_pairs={{32,0},{40,8},{48,16},{56,24},{64,32},{72,40},{80,48},{88,56},{96,... | collective-permute-start | bytes 245768 | tf_op jit(solution)/shard_map/ppermute | solution.py:19
  96.0 19.0 %collective-permute-start.14 = (f32[1,2,20,2,256]{4,3,2,1,0:T(2,128)S(1)}, f32[1,2,20,2,256]{4,3,2,1,0:T(2,128)S(1)}, u32[]{:S(2)}, u32[]{:S(2)}) collective-permute-start(f32[1,2,20,2,256]{4,3,2,1,0:T(2,128)S(1)} %get-tuple-element.86), channel_id=1, source_target_pairs={{0,32},{8,40},{16,48},{24,56},{32,64},{40,72},{48,80},{56,88},{64,... | collective-permute-start | bytes 245768 | tf_op jit(solution)/shard_map/ppermute | solution.py:19
  115.3 25.4 %collective-permute-start.17 = (f32[1,2,20,12,2]{4,3,2,1,0:T(8,128)S(1)}, f32[1,2,20,12,2]{4,3,2,1,0:T(8,128)S(1)}, u32[]{:S(2)}, u32[]{:S(2)}) collective-permute-start(f32[1,2,20,12,2]{4,3,2,1,0:T(8,128)S(1)} %get-tuple-element.77), channel_id=1, source_target_pairs={{128,0},{136,8},{144,16},{152,24},{160,32},{168,40},{176,48},{184,... | collective-permute-start | bytes 11528 | tf_op jit(solution)/shard_map/ppermute | solution.py:19
  116.6 26.1 %collective-permute-start.16 = (f32[1,2,20,12,2]{4,3,2,1,0:T(8,128)S(1)}, f32[1,2,20,12,2]{4,3,2,1,0:T(8,128)S(1)}, u32[]{:S(2)}, u32[]{:S(2)}) collective-permute-start(f32[1,2,20,12,2]{4,3,2,1,0:T(8,128)S(1)} %get-tuple-element.76), channel_id=1, source_target_pairs={{0,128},{8,136},{16,144},{24,152},{32,160},{40,168},{48,176},{56,1... | collective-permute-start | bytes 11528 | tf_op jit(solution)/shard_map/ppermute | solution.py:19
  150.8 5.4 %collective-permute-start.19 = (f32[1,2,1,8,256]{4,3,2,1,0:T(8,128)S(1)}, f32[1,2,1,8,256]{4,3,2,1,0:T(8,128)S(1)}, u32[]{:S(2)}, u32[]{:S(2)}) collective-permute-start(f32[1,2,1,8,256]{4,3,2,1,0:T(8,128)S(1)} %get-tuple-element.73), channel_id=1, source_target_pairs={{8,0},{16,8},{24,16},{32,24},{40,32},{48,40},{56,48},{64,56},{72,6... | collective-permute-start | bytes 49160 | tf_op jit(solution)/shard_map/ppermute | solution.py:19
  157.1 10.2 %collective-permute-start.21 = (f32[1,2,18,1,256]{4,3,2,1,0:T(1,128)S(1)}, f32[1,2,18,1,256]{4,3,2,1,0:T(1,128)S(1)}, u32[]{:S(2)}, u32[]{:S(2)}) collective-permute-start(f32[1,2,18,1,256]{4,3,2,1,0:T(1,128)S(1)} %get-tuple-element.89), channel_id=1, source_target_pairs={{32,0},{40,8},{48,16},{56,24},{64,32},{72,40},{80,48},{88,56},{96,... | collective-permute-start | bytes 110600 | tf_op jit(solution)/shard_map/ppermute | solution.py:19
  158.4 9.9 %collective-permute-start.20 = (f32[1,2,18,1,256]{4,3,2,1,0:T(1,128)S(1)}, f32[1,2,18,1,256]{4,3,2,1,0:T(1,128)S(1)}, u32[]{:S(2)}, u32[]{:S(2)}) collective-permute-start(f32[1,2,18,1,256]{4,3,2,1,0:T(1,128)S(1)} %get-tuple-element.88), channel_id=1, source_target_pairs={{0,32},{8,40},{16,48},{24,56},{32,64},{40,72},{48,80},{56,88},{64,... | collective-permute-start | bytes 110600 | tf_op jit(solution)/shard_map/ppermute | solution.py:19
  168.6 20.3 %collective-permute-start.23 = (f32[1,2,18,10,1]{4,3,2,1,0:T(8,128)S(1)}, f32[1,2,18,10,1]{4,3,2,1,0:T(8,128)S(1)}, u32[]{:S(2)}, u32[]{:S(2)}) collective-permute-start(f32[1,2,18,10,1]{4,3,2,1,0:T(8,128)S(1)} %get-tuple-element.79), channel_id=1, source_target_pairs={{128,0},{136,8},{144,16},{152,24},{160,32},{168,40},{176,48},{184,... | collective-permute-start | bytes 4328 | tf_op jit(solution)/shard_map/ppermute | solution.py:19
  170.1 20.5 %collective-permute-start.22 = (f32[1,2,18,10,1]{4,3,2,1,0:T(8,128)S(1)}, f32[1,2,18,10,1]{4,3,2,1,0:T(8,128)S(1)}, u32[]{:S(2)}, u32[]{:S(2)}) collective-permute-start(f32[1,2,18,10,1]{4,3,2,1,0:T(8,128)S(1)} %get-tuple-element.78), channel_id=1, source_target_pairs={{0,128},{8,136},{16,144},{24,152},{32,160},{40,168},{48,176},{56,1... | collective-permute-start | bytes 4328 | tf_op jit(solution)/shard_map/ppermute | solution.py:19
  234.3 24.0 %all-to-all-start.1 = ((f32[8,2,8,256]{3,2,1,0:T(8,128)}), f32[8,2,8,256]{3,2,1,0:T(8,128)S(1)}, u32[]{:S(2)}, u32[]{:S(2)}) async-start(f32[8,2,8,256]{3,2,1,0:T(8,128)} %bitcast.87), calls=%async_computation.1 | async-start | bytes 262144 | tf_op jit(solution)/shard_map/all_to_all | solution.py:173
  (9 other events, 202.7 us)

commit v2 on v0

v2 whole, which is shorter than its diff:
```python
import jax
import jax.numpy as jnp
from jax import lax
from jax.experimental import pallas as pl
from jax.experimental.pallas import tpu as pltpu
from jax.sharding import PartitionSpec as P

SWEEPS = 4
PX = 4
PY = 4
PZ = 4
CX = 16
CY = 8
CZ = 256
CENTER = 13.5
RELAX = 0.7

SCALE = 16.0
MIDDLE = 4.0
PIVOT = 64.0

GROUP = PX * PY
SLAB = CZ // GROUP
DEEP = 8
THICK = SLAB + 2 * DEEP
LANES = 128
TILE = 8

PLANES = CX + 4
SLOT = CY + 3
SLOTS = 6
TILES = 9
BASE = 8
ROWS = BASE + TILES * TILE + 8
BODY = slice(BASE, BASE + TILES * TILE)
WIDE = 40
OWN = 11
FIELDS = 4
STATS = 8
BACK = FIELDS * SLAB + STATS
UNROLL = 3
VMEM_LIMIT = 48 * 1024 * 1024


def slot_of(unit):
    i, j = unit % PX, unit // PX
    if i < PX - 1:
        return j, i
    return (PX, j) if j < PY - 1 else (PX + 1, 0)


def first_row(slot):
    return BASE + SLOT * slot


def lanes_of(values):
    return lax.broadcasted_iota(jnp.int32, values.shape, values.ndim - 1)


def turn_kernel(source_ref, kappa_ref, damping_ref, own_ref, low_ref, high_ref):
    for field in range(FIELDS):
        for tile in range(CZ // LANES):
            here = slice(tile * LANES, (tile + 1) * LANES)
            if field < 2:
                values = source_ref[field, :, :, here]
            else:
                values = (kappa_ref, damping_ref)[field - 2][:, :, here]
            own_ref[field, here] = values.reshape(LANES, LANES).T
        low_ref[field] = own_ref[field, 0:DEEP]
        high_ref[field] = own_ref[field, CZ - DEEP:CZ]


def message_kernel(own_ref, below_ref, above_ref, out_ref):
    for field in range(FIELDS):
        for target in range(GROUP):
            first = target * SLAB - DEEP
            low = max(first, 0)
            high = min(first + THICK, CZ)
            out_ref[target, field, low - first:high - first] = own_ref[field, low:high]
        out_ref[0, field, 0:DEEP] = below_ref[field]
        out_ref[GROUP - 1, field, THICK - DEEP:THICK] = above_ref[field]


def total(values):
    return jnp.sum(jnp.sum(values, axis=0, keepdims=True), axis=1, keepdims=True)


def solve_kernel(got_ref, back_ref, r_ref, w_ref, d_ref, z_ref, y_ref, q_ref, u_ref, turn_ref, turned_ref):
    place = lax.rem(lax.axis_index("sub"), GROUP)
    is_first = place == 0
    is_last = place == GROUP - 1
    low_at = jnp.where(is_first, 0, 3)
    high_at = jnp.where(is_last, 30, 27)

    turn_ref[...] = jnp.zeros_like(turn_ref)
    for ref in (r_ref, w_ref, d_ref):
        @pl.loop(0, PLANES)
        def _(plane):
            for part in range(2):
                ref[part, plane] = jnp.zeros((ROWS, LANES), jnp.float32)
    for ref in (z_ref, y_ref):
        for part in range(2):
            ref[part, :, 0:BASE] = jnp.zeros((PLANES, BASE, LANES), jnp.float32)
            ref[part, :, ROWS - 8:ROWS] = jnp.zeros((PLANES, 8, LANES), jnp.float32)
    for part in range(2):
        for plane in (0, PLANES - 1):
            u_ref[part, plane] = jnp.zeros((ROWS, LANES), jnp.float32)
        for plane in (1, PLANES - 2):
            q_ref[part, plane] = jnp.zeros((ROWS, LANES), jnp.float32)

    for unit in range(GROUP):
        slot, group = slot_of(unit)
        at = group * WIDE
        for field in range(FIELDS):
            turn_ref[slot, field, pl.ds(at + low_at, DEEP)] = got_ref[unit, field, 0:DEEP]
            turn_ref[slot, field, at + OWN:at + OWN + SLAB] = got_ref[unit, field, DEEP:DEEP + SLAB]
            turn_ref[slot, field, pl.ds(at + high_at, DEEP)] = got_ref[unit, field, DEEP + SLAB:THICK]

    def fix(targets):
        for unit in range(GROUP):
            slot, group = slot_of(unit)
            at = group * WIDE
            for field in range(FIELDS):
                for target, source in targets:
                    if source is None:
                        row = jnp.zeros((1, LANES), jnp.float32)
                    else:
                        row = got_ref[unit, field, source:source + 1]
                    turn_ref[slot, field, at + target:at + target + 1] = row

    @pl.when(is_first)
    def _():
        fix(((8, DEEP), (9, None), (10, DEEP - 1)))

    @pl.when(is_last)
    def _():
        fix(((27, DEEP + SLAB), (28, None), (29, DEEP + SLAB - 1)))

    for slot in range(SLOTS):
        for field in range(FIELDS):
            turned_ref[slot, field] = turn_ref[slot, field].T

    @pl.loop(0, CX)
    def _(plane):
        at = pl.ds(pl.multiple_of(plane * TILE, TILE), TILE)
        for slot in range(SLOTS):
            b_re, b_im, kappa, damping = [turned_ref[slot, field, at] for field in range(FIELDS)]
            rows = slice(first_row(slot) + 1, first_row(slot) + 1 + CY)
            d_re = CENTER - kappa
            d_im = kappa * damping
            p_re = d_re - MIDDLE
            factor = jnp.where(kappa > 0, (RELAX / SCALE) / (p_re * p_re + d_im * d_im), 0.0)
            r_ref[0, 2 + plane, rows] = SCALE * b_re
            r_ref[1, 2 + plane, rows] = SCALE * b_im
            w_ref[0, 2 + plane, rows] = factor * p_re
            w_ref[1, 2 + plane, rows] = -factor * d_im
            d_ref[0, 2 + plane, rows] = SCALE * d_re
            d_ref[1, 2 + plane, rows] = SCALE * d_im

    def swap_ends(ref):
        def run(pairs):
            @pl.loop(2, 2 + CX)
            def _(plane):
                for part in range(2):
                    values = ref[part, plane, BODY]
                    lane = lax.rem(lanes_of(values), WIDE)
                    up = pltpu.roll(values, 3, 1)
                    down = pltpu.roll(values, LANES - 3, 1)
                    (a, b) = pairs
                    ref[part, plane, BODY] = jnp.where(lane == a, down, jnp.where(lane == b, up, values))

        @pl.when(is_first)
        def _():
            run((8, 10))

        @pl.when(is_last)
        def _():
            run((27, 29))

    def swap_sides(ref):
        one = jnp.zeros((TILE, LANES), jnp.float32)
        lane = lanes_of(one)
        last, first = CX + 1, 2

        def rows(slot):
            return slice(first_row(slot) + 1, first_row(slot) + 1 + CY)

        for part in range(2):
            for j in range(PY):
                here = rows(j)
                moved_up = pltpu.roll(ref[part, last, here], WIDE, 1)
                ref[part, 1, here] = jnp.where((lane >= WIDE) & (lane < 3 * WIDE), moved_up, ref[part, 1, here])
                slot, group = slot_of(PX - 1 + PX * j)
                end = rows(slot)
                inside = (lane >= group * WIDE) & (lane < (group + 1) * WIDE)
                shift = (2 - group) * WIDE
                moved_down = pltpu.roll(ref[part, first, here], LANES - WIDE, 1)
                from_end = pltpu.roll(ref[part, first, end], shift, 1) if shift else ref[part, first, end]
                ref[part, PLANES - 2, here] = jnp.where(
                    lane < 2 * WIDE, moved_down, jnp.where(lane < 3 * WIDE, from_end, ref[part, PLANES - 2, here]))
                to_end = ref[part, last, here]
                to_end = pltpu.roll(to_end, LANES - shift, 1) if shift else to_end
                ref[part, 1, end] = jnp.where(inside, to_end, ref[part, 1, end])

        def across(plane):
            for part in range(2):
                def row(slot, n):
                    return slice(first_row(slot) + n, first_row(slot) + n + 1)

                for j in range(PY):
                    if j > 0:
                        ref[part, plane, row(j, 0)] = ref[part, plane, row(j - 1, CY)]
                    if j < PY - 1:
                        ref[part, plane, row(j, CY + 1)] = ref[part, plane, row(j + 1, 1)]
                top = ref[part, plane, row(4, CY)]
                bottom = ref[part, plane, row(4, 1)]
                extra = ref[part, plane, row(5, 1)]
                lane = lanes_of(top)
                old = ref[part, plane, row(4, 0)]
                ref[part, plane, row(4, 0)] = jnp.where(
                    (lane >= WIDE) & (lane < 3 * WIDE), pltpu.roll(top, WIDE, 1), old)
                old = ref[part, plane, row(4, CY + 1)]
                ref[part, plane, row(4, CY + 1)] = jnp.where(
                    lane < 2 * WIDE, pltpu.roll(bottom, LANES - WIDE, 1),
                    jnp.where(lane < 3 * WIDE, pltpu.roll(extra, 2 * WIDE, 1), old))
                old = ref[part, plane, row(5, 0)]
                ref[part, plane, row(5, 0)] = jnp.where(lane < WIDE, pltpu.roll(top, LANES - 2 * WIDE, 1), old)

        loop(1, PLANES - 1, across)

    def loop(first, last, body):
        def step(plane, carry):
            body(plane)
            return carry

        lax.fori_loop(first, last, step, 0, unroll=UNROLL)

    swap_sides(r_ref)
    swap_sides(w_ref)

    def mix(ref, plane):
        for part in range(2):
            for t in range(TILES):
                at = BASE + t * TILE
                here = ref[part, plane, at:at + TILE]
                mixed = ref[part, plane, at - 1:at + TILE - 1] + ref[part, plane, at + 1:at + TILE + 1] + MIDDLE * here
                u_ref[part, plane, at:at + TILE] = (
                    pltpu.roll(mixed, 1, 1) + pltpu.roll(mixed, LANES - 1, 1) + MIDDLE * mixed)

    def smoothed(part, plane, at):
        return u_ref[part, plane - 1, at] + u_ref[part, plane + 1, at] + MIDDLE * u_ref[part, plane, at]

    def tiles():
        return [slice(BASE + t * TILE, BASE + (t + 1) * TILE) for t in range(TILES)]

    def sweep(ref, first, last, body):
        for plane in range(1, first + 2):
            mix(ref, plane)

        def step(plane):
            body(plane)
            mix(ref, plane + 2)

        loop(first, PLANES - 3, step)
        for plane in range(PLANES - 3, last + 1):
            body(plane)

    def precondition(ref, right_ref):
        def start(plane):
            for at in tiles():
                r_re, r_im = right_ref[0, plane, at], right_ref[1, plane, at]
                w_re, w_im = w_ref[0, plane, at], w_ref[1, plane, at]
                ref[0, plane, at] = w_re * r_re - w_im * r_im
                ref[1, plane, at] = w_re * r_im + w_im * r_re

        def update(plane):
            for at in tiles():
                z_re, z_im = ref[0, plane, at], ref[1, plane, at]
                w_re, w_im = w_ref[0, plane, at], w_ref[1, plane, at]
                g_re = (right_ref[0, plane, at] + smoothed(0, plane, at)) - PIVOT * z_re
                g_im = (right_ref[1, plane, at] + smoothed(1, plane, at)) - PIVOT * z_im
                ref[0, plane, at] = (1.0 - RELAX) * z_re + (w_re * g_re - w_im * g_im)
                ref[1, plane, at] = (1.0 - RELAX) * z_im + (w_re * g_im + w_im * g_re)

        loop(1, PLANES - 1, start)
        for number in range(1, SWEEPS):
            final = number == SWEEPS - 1
            sweep(ref, 2 if final else 1, PLANES - 3 if final else PLANES - 2, update)
        swap_ends(ref)
        swap_sides(ref)

    def image(ref, out_ref):
        def body(plane):
            for at in tiles():
                z_re, z_im = ref[0, plane, at], ref[1, plane, at]
                d_re, d_im = d_ref[0, plane, at], d_ref[1, plane, at]
                out_ref[0, plane, at] = (d_re * z_re - d_im * z_im) - smoothed(0, plane, at)
                out_ref[1, plane, at] = (d_re * z_im + d_im * z_re) - smoothed(1, plane, at)

        sweep(ref, 2, PLANES - 3, body)

    precondition(z_ref, r_ref)
    image(z_ref, q_ref)
    swap_ends(q_ref)
    swap_sides(q_ref)
    precondition(y_ref, q_ref)
    image(y_ref, w_ref)

    def own_cells(t):
        shape = (TILE, LANES)
        row = lax.broadcasted_iota(jnp.int32, shape, 0) + t * TILE
        lane = lax.broadcasted_iota(jnp.int32, shape, 1)
        y = lax.rem(row, SLOT)
        z = lax.rem(lane, WIDE)
        inside = (y >= 1) & (y <= CY) & (z >= OWN) & (z < OWN + SLAB)
        return inside & ((row < 5 * SLOT) & (lane < 3 * WIDE) | (row < SLOTS * SLOT) & (lane < WIDE))

    zero = jnp.zeros((TILE, LANES), jnp.float32)

    def first_sums(plane, sums):
        norm, proj_re, proj_im, cross_re, cross_im = sums
        for t, at in enumerate(tiles()):
            keep = own_cells(t)
            q_re = jnp.where(keep, q_ref[0, plane, at], 0.0)
            q_im = jnp.where(keep, q_ref[1, plane, at], 0.0)
            b_re, b_im = r_ref[0, plane, at], r_ref[1, plane, at]
            t_re, t_im = w_ref[0, plane, at], w_ref[1, plane, at]
            norm = norm + (q_re * q_re + q_im * q_im)
            proj_re = proj_re + (q_re * b_re + q_im * b_im)
            proj_im = proj_im + (q_re * b_im - q_im * b_re)
            cross_re = cross_re + (q_re * t_re + q_im * t_im)
            cross_im = cross_im + (q_re * t_im - q_im * t_re)
        return norm, proj_re, proj_im, cross_re, cross_im

    sums = lax.fori_loop(2, 2 + CX, first_sums, (zero,) * 5, unroll=2)
    norm, proj_re, proj_im, cross_re, cross_im = [total(v) for v in sums]
    safe = jnp.where(norm > 0, norm, 1.0)
    cross_re = cross_re / safe
    cross_im = cross_im / safe

    def second_sums(plane, sums):
        rest, pair_re, pair_im = sums
        for t, at in enumerate(tiles()):
            keep = own_cells(t)
            q_re, q_im = q_ref[0, plane, at], q_ref[1, plane, at]
            b_re, b_im = r_ref[0, plane, at], r_ref[1, plane, at]
            p_re = jnp.where(keep, w_ref[0, plane, at] - (cross_re * q_re - cross_im * q_im), 0.0)
            p_im = jnp.where(keep, w_ref[1, plane, at] - (cross_re * q_im + cross_im * q_re), 0.0)
            rest = rest + (p_re * p_re + p_im * p_im)
            pair_re = pair_re + (p_re * b_re + p_im * b_im)
            pair_im = pair_im + (p_re * b_im - p_im * b_re)
        return rest, pair_re, pair_im

    rest, pair_re, pair_im = [total(v) for v in lax.fori_loop(2, 2 + CX, second_sums, (zero,) * 3, unroll=2)]
    row = lax.broadcasted_iota(jnp.int32, (STATS, LANES), 0)
    table = jnp.zeros((STATS, LANES), jnp.float32)
    for n, value in enumerate((norm, proj_re, proj_im, cross_re, cross_im, rest, pair_re, pair_im)):
        table = jnp.where(row == n, value, table)

    for unit in range(GROUP):
        back_ref[unit, FIELDS * SLAB:BACK] = table
    for field in range(FIELDS):
        ref, part = (z_ref, y_ref)[field // 2], field % 2
        for slot in range(SLOTS):
            rows = slice(first_row(slot) + 1, first_row(slot) + 1 + CY)
            turned = ref[part, 2:2 + CX, rows].reshape(LANES, LANES).T
            for unit in range(GROUP):
                if slot_of(unit)[0] == slot:
                    at = slot_of(unit)[1] * WIDE + OWN
                    back_ref[unit, field * SLAB:(field + 1) * SLAB] = turned[at:at + SLAB]


def merged(rows):
    norm, proj_re, proj_im, cross_re, cross_im, rest, pair_re, pair_im = rows

    def over(values):
        return jnp.sum(values, axis=0, keepdims=True)

    whole = over(norm)
    mean_re = over(norm * cross_re) / whole
    mean_im = over(norm * cross_im) / whole
    off_re = cross_re - mean_re
    off_im = cross_im - mean_im
    return (whole, over(proj_re), over(proj_im), mean_re, mean_im,
            over(rest + norm * (off_re * off_re + off_im * off_im)),
            over(pair_re + off_re * proj_re + off_im * proj_im),
            over(pair_im + off_re * proj_im - off_im * proj_re))


def merge_kernel(back_ref, out_ref):
    rows = [back_ref[:, FIELDS * SLAB + n] for n in range(STATS)]
    for n, value in enumerate(merged(rows)):
        for target in range(PZ):
            out_ref[target, n:n + 1] = value


def finish_kernel(table_ref, back_ref, wave_ref, damping_ref, solution_ref, shares_ref):
    norm, proj_re, proj_im, mean_re, mean_im, size, pair_re, pair_im = merged([table_ref[:, n] for n in range(STATS)])
    beta_re = pair_re / size
    beta_im = pair_im / size
    lead_re = proj_re / norm - (beta_re * mean_re - beta_im * mean_im)
    lead_im = proj_im / norm - (beta_re * mean_im + beta_im * mean_re)
    shape = (SLAB, LANES)
    beta_re, beta_im, lead_re, lead_im = [jnp.broadcast_to(v, shape) for v in (beta_re, beta_im, lead_re, lead_im)]
    per = LANES // SLAB
    for tile in range(CZ // LANES):
        pieces = [[], []]
        for source in range(tile * per, (tile + 1) * per):
            f_re, f_im, s_re, s_im = [back_ref[source, n * SLAB:(n + 1) * SLAB] for n in range(FIELDS)]
            pieces[0].append((lead_re * f_re - lead_im * f_im) + (beta_re * s_re - beta_im * s_im))
            pieces[1].append((lead_re * f_im + lead_im * f_re) + (beta_re * s_im + beta_im * s_re))
        here = slice(tile * LANES, (tile + 1) * LANES)
        x_re, x_im = [jnp.concatenate(p, axis=0).T.reshape(CX, CY, LANES) for p in pieces]
        solution_ref[0, :, :, here] = x_re
        solution_ref[1, :, :, here] = x_im
        u_re, u_im = wave_ref[0, :, :, here], wave_ref[1, :, :, here]
        shares_ref[:, :, here] = (u_re * x_re + u_im * x_im) - damping_ref[:, :, here] * (u_im * x_re - u_re * x_im)


def moved(values, stride):
    steps = PX * PY * PZ
    pairs = []
    for index in range(steps):
        place = index // abs(stride) % 4 + (1 if stride > 0 else -1)
        if 0 <= place < 4:
            pairs.append((index, index + stride))
    return lax.ppermute(values, "sub", pairs)


def call(kernel, out_shapes, scratch=()):
    one = pl.BlockSpec(memory_space=pltpu.VMEM)

    def run(*args):
        return pl.pallas_call(
            kernel,
            out_shape=[jax.ShapeDtypeStruct(shape, jnp.float32) for shape in out_shapes],
            in_specs=[one] * len(args),
            out_specs=[one] * len(out_shapes),
            scratch_shapes=list(scratch),
            compiler_params=pltpu.CompilerParams(vmem_limit_bytes=VMEM_LIMIT),
        )(*args)

    return run


def local(adjoint_source, forward_field, kappa, damping):
    source = adjoint_source[0, :, 0]
    wave = forward_field[0, :, 0]
    kappa = kappa[0]
    damping = damping[0]
    face = (FIELDS, DEEP, LANES)
    own, low, high = call(turn_kernel, [(FIELDS, CZ, LANES), face, face])(source, kappa, damping)
    below = moved(high, PX * PY)
    above = moved(low, -PX * PY)
    message, = call(message_kernel, [(GROUP, FIELDS, THICK, LANES)])(own, below, above)
    layers = [[k * GROUP + n for n in range(GROUP)] for k in range(PZ)]
    columns = [[k * GROUP + n for k in range(PZ)] for n in range(GROUP)]
    got = lax.all_to_all(message, "sub", 0, 0, axis_index_groups=layers)
    work = pltpu.VMEM((2, PLANES, ROWS, LANES), jnp.float32)
    turn = pltpu.VMEM((SLOTS, FIELDS, LANES, LANES), jnp.float32)
    back, = call(solve_kernel, [(GROUP, BACK, LANES)], [work] * 7 + [turn] * 2)(got)
    back = lax.all_to_all(back, "sub", 0, 0, axis_index_groups=layers)
    part, = call(merge_kernel, [(PZ, STATS, LANES)])(back)
    table = lax.all_to_all(part, "sub", 0, 0, axis_index_groups=columns)
    solved, shares = call(finish_kernel, [(2, CX, CY, CZ), (CX, CY, CZ)])(table, back, wave, damping)
    shots = lax.axis_size("shot")
    shares = shares.reshape(shots, CX // shots, CY, CZ)
    share = jnp.sum(lax.all_to_all(shares, "shot", 0, 0), axis=0)
    return (solved[None, :, None], share[None])


def solution(mesh):
    return jax.shard_map(
        local,
        mesh=mesh,
        in_specs=(
            P("shot", None, "sub", None, None, None),
            P("shot", None, "sub", None, None, None),
            P("sub", None, None, None),
            P("sub", None, None, None),
        ),
        out_specs=(P("shot", None, "sub", None, None, None), P("sub", "shot", None, None)),
        check_vma=False,
    )
```

time: 984 us -> 126 us (0.13)
  blocking collectives: 569 us -> 89.6 us
  waiting for transfers between devices: 186 us -> 3.18 us
  starting transfers between devices: 165 us -> 5.24 us
  other arithmetic: 30.4 us -> 0.62 us
  Pallas kernels: 0 us -> 23.8 us
  between operations: 23.1 us -> 0.69 us
    psum x3 -> x0, blocking collectives: 569 us -> none  [the longest x1 191 us: local(): lax.psum((squares(first_img), local_re, local_im), 'sub')]
    psum x1 -> x0, waiting for transfers between devices: 164 us -> none  [local(): summed = lax.psum(partial_terms, 'shot')]
    ppermute x30 -> x2, starting transfers between devices: 165 us -> 5.24 us  [moved(): return lax.ppermute(values, 'sub', pairs)]
    all_to_all x0 -> x4, blocking collectives: none -> 89.6 us  [the longest x1 42.9 us: local(): got = lax.all_to_all(message, 'sub', 0, 0, axis_index_groups=layers)]
    pallas_call x0 -> x5, Pallas kernels: none -> 23.8 us  [run(): pl.pallas_call(kernel, out_shape=[jax.ShapeDtypeStruct(shape, jnp.float32...]
    ppermute x30 -> x2, waiting for transfers between devices: 21.9 us -> 3.18 us  [moved(): return lax.ppermute(values, 'sub', pairs)]
    sub x14 -> x0, other arithmetic: 10 us -> none  [the longest x6 6.77 us: sweeps(): defect = extended - (cmul(framed[0], framed[1], approx) - smooth(approx))]
  transfers between devices with their start and end apart: 31 -> 2, of which waited for: 15 -> 1; matrix products, arithmetic and copies ran while one was open for 1% -> 0% of each run, Pallas kernels for 0% -> 0%
where the time goes in v2:
time: 126 us
  blocking collectives  89.6 us (71%)
  Pallas kernels  23.8 us (19%)
  starting transfers between devices  5.24 us (4%)
  waiting for transfers between devices  3.18 us (3%)
  local copies, waits for them, and re-layouts  2.76 us (2%)
    all_to_all x1, blocking collectives, local(): got = lax.all_to_all(message, 'sub', 0, 0, axis_index_groups=layers)  42.9 us
    pallas_call x5, Pallas kernels, run(): pl.pallas_call(kernel, out_shape=[jax.ShapeDtypeStruct(shape, jnp.float32...  23.8 us
    all_to_all x1, blocking collectives, local(): back = lax.all_to_all(back, 'sub', 0, 0, axis_index_groups=layers)  23.2 us
    all_to_all x1, blocking collectives, local(): share = jnp.sum(lax.all_to_all(shares, 'shot', 0, 0), axis=0)  15.7 us
    all_to_all x1, blocking collectives, local(): table = lax.all_to_all(part, 'sub', 0, 0, axis_index_groups=columns)  7.87 us
    ppermute x2, starting transfers between devices, moved(): return lax.ppermute(values, 'sub', pairs)  5.24 us
    ppermute x2, waiting for transfers between devices, moved(): return lax.ppermute(values, 'sub', pairs)  3.18 us
    unnamed x10, local copies, waits for them, and re-layouts  2.76 us
  transfers between devices with their start and end apart: 2, of which 1 were waited for; matrix products, arithmetic and copies ran while one was open for 0% of the time, Pallas kernels for 0%

profile of v2, /device:TPU:1, one launch (start us, length us, event | category | flops | bytes accessed | tf_op | source)
XLA Modules:
  0.0 125.9 jit_solution(3843294322184303286)
XLA Ops:
  0.6 0.0 copy-start
  0.6 0.9 copy-done
  1.5 0.0 copy-start.2
  1.5 0.9 copy-done.2
  2.5 0.0 copy-start.4
  2.5 0.9 copy-done.4
  3.4 0.2 shard_map.59
  3.6 3.9 %collective-permute-start = (f32[4,8,128]{2,1,0:T(8,128)S(1)}, f32[4,8,128]{2,1,0:T(8,128)S(1)}, u32[]{:S(2)}, u32[]{:S(2)}) collective-permute-start(f32[4,8,128]{2,1,0:T(8,128)S(1)} %get-tuple-element.8), channel_id=1, source_target_pairs={{0,128},{8,136},{16,144},{24,152},{32,160},{40,168},{48,176},{56,1... | collective-permute-start | bytes 49160 | tf_op jit(solution)/shard_map/ppermute | solution.py:427
  7.5 1.3 %collective-permute-start.1 = (f32[4,8,128]{2,1,0:T(8,128)S(1)}, f32[4,8,128]{2,1,0:T(8,128)S(1)}, u32[]{:S(2)}, u32[]{:S(2)}) collective-permute-start(f32[4,8,128]{2,1,0:T(8,128)S(1)} %get-tuple-element.9), channel_id=1, source_target_pairs={{128,0},{136,8},{144,16},{152,24},{160,32},{168,40},{176,48},{184,... | collective-permute-start | bytes 49160 | tf_op jit(solution)/shard_map/ppermute | solution.py:427
  8.8 0.0 collective-permute-done.below_ref
  8.9 3.2 %collective-permute-done.1.above_ref = f32[4,8,128]{2,1,0:T(8,128)S(1)} collective-permute-done((f32[4,8,128]{2,1,0:T(8,128)S(1)}, f32[4,8,128]{2,1,0:T(8,128)S(1)}, u32[]{:S(2)}, u32[]{:S(2)}) %collective-permute-start.1) | collective-permute-done | bytes 16416 | tf_op jit(solution)/shard_map/ppermute | solution.py:427
  12.0 0.1 shard_map.60
  12.1 42.9 %all_to_all.20.got_ref = f32[16,4,32,128]{3,2,1,0:T(8,128)S(1)} all-to-all(f32[16,4,32,128]{3,2,1,0:T(8,128)S(1)} %shard_map.60), channel_id=1, replica_groups={{0,8,16,24,32,40,48,56,64,72,80,88,96,104,112,120},{128,136,144,152,160..., dimensions={0} | all-to-all | bytes 2097152 | tf_op jit(solution)/shard_map/all_to_all | solution.py:458
  55.0 22.6 %shard_map.61 = f32[16,72,128]{2,1,0:T(8,128)S(1)} custom-call(f32[16,4,32,128]{3,2,1,0:T(8,128)S(1)} %all_to_all.20.got_ref), custom_call_target="tpu_custom_call" | custom-call | tf_op jit(solution)/shard_map/pallas_call | solution.py:434
  77.6 23.2 %all_to_all.21.back_ref = f32[16,72,128]{2,1,0:T(8,128)S(1)} all-to-all(f32[16,72,128]{2,1,0:T(8,128)S(1)} %shard_map.61), channel_id=1, replica_groups={{0,8,16,24,32,40,48,56,64,72,80,88,96,104,112,120},{128,136,144,152,160..., dimensions={0} | all-to-all | bytes 1179648 | tf_op jit(solution)/shard_map/all_to_all | solution.py:462
  100.8 0.0 copy-start.1
  100.8 0.0 copy-start.3
  100.8 0.1 shard_map.62
  100.9 7.9 %all_to_all.22.table_ref = f32[4,8,128]{2,1,0:T(8,128)S(1)} all-to-all(f32[4,8,128]{2,1,0:T(8,128)S(1)} %shard_map.62), channel_id=1, replica_groups={{0,128,256,384},{8,136,264,392},{16,144,272,400},{24,152,280,408},{32,1..., dimensions={0} | all-to-all | bytes 32768 | tf_op jit(solution)/shard_map/all_to_all | solution.py:464
  108.7 0.0 copy-done.1
  108.7 0.0 copy-done.3
  108.7 0.9 shard_map.63
  109.6 15.7 %all_to_all.23 = f32[8,2,8,256]{3,2,1,0:T(8,128)S(1)} all-to-all(f32[8,2,8,256]{3,2,1,0:T(8,128)S(1)} %bitcast.13), channel_id=1, replica_groups=mesh['sub'=64,'shot'=8] {'shot'}, dimensions={0} | all-to-all | bytes 262144 | tf_op jit(solution)/shard_map/all_to_all | solution.py:468
  125.3 0.6 reduce_sum.9
Async XLA Ops:
  0.6 0.9 copy-start
  1.5 0.9 copy-start.2
  2.5 0.9 copy-start.4
  3.6 5.3 %collective-permute-start = (f32[4,8,128]{2,1,0:T(8,128)S(1)}, f32[4,8,128]{2,1,0:T(8,128)S(1)}, u32[]{:S(2)}, u32[]{:S(2)}) collective-permute-start(f32[4,8,128]{2,1,0:T(8,128)S(1)} %get-tuple-element.8), channel_id=1, source_target_pairs={{0,128},{8,136},{16,144},{24,152},{32,160},{40,168},{48,176},{56,1... | collective-permute-start | bytes 49160 | tf_op jit(solution)/shard_map/ppermute | solution.py:427
  7.5 4.5 %collective-permute-start.1 = (f32[4,8,128]{2,1,0:T(8,128)S(1)}, f32[4,8,128]{2,1,0:T(8,128)S(1)}, u32[]{:S(2)}, u32[]{:S(2)}) collective-permute-start(f32[4,8,128]{2,1,0:T(8,128)S(1)} %get-tuple-element.9), channel_id=1, source_target_pairs={{128,0},{136,8},{144,16},{152,24},{160,32},{168,40},{176,48},{184,... | collective-permute-start | bytes 49160 | tf_op jit(solution)/shard_map/ppermute | solution.py:427
  100.8 8.0 %copy-start.1 = (f32[1,16,8,256]{3,2,1,0:T(8,128)S(1)}, f32[1,16,8,256]{3,2,1,0:T(8,128)}, u32[]{:S(2)}) copy-start(f32[1,16,8,256]{3,2,1,0:T(8,128)} %param.7) | copy-start | bytes 393220
  100.8 8.0 %copy-start.3 = (f32[1,2,1,16,8,256]{5,4,3,2,1,0:T(8,128)S(1)}, f32[1,2,1,16,8,256]{5,4,3,2,1,0:T(8,128)}, u32[]{:S(2)}) copy-start(f32[1,2,1,16,8,256]{5,4,3,2,1,0:T(8,128)} %param.5) | copy-start | bytes 786436

commit v3 on v2

v3 whole, which is shorter than its diff:
```python
import jax
import jax.numpy as jnp
from jax import lax
from jax.experimental import pallas as pl
from jax.experimental.pallas import tpu as pltpu
from jax.sharding import PartitionSpec as P

SWEEPS = 4
PX = 4
PY = 4
PZ = 4
CX = 16
CY = 8
CZ = 256
CENTER = 13.5
RELAX = 0.7

SCALE = 16.0
MIDDLE = 4.0
PIVOT = 64.0

GROUP = PX * PY
SLAB = CZ // GROUP
RING = GROUP // 2
DEEP = 8
LANES = 128
TILE = 8

PLANES = CX + 4
SLOT = CY + 3
SLOTS = 6
TILES = 9
BASE = 8
ROWS = BASE + TILES * TILE + 8
BODY = slice(BASE, BASE + TILES * TILE)
WIDE = 40
OWN = 11
FIELDS = 4
STATS = 8
BACK = FIELDS * SLAB + STATS
VMEM_LIMIT = 24 * 1024 * 1024


def slot_of(unit):
    i, j = unit % PX, unit // PX
    if i < PX - 1:
        return j, i
    return (PX, j) if j < PY - 1 else (PX + 1, 0)


def first_row(slot):
    return BASE + SLOT * slot


def lanes_of(values):
    return lax.broadcasted_iota(jnp.int32, values.shape, values.ndim - 1)


def turn_kernel(source_ref, kappa_ref, damping_ref, out_ref, source_held, kappa_held, damping_held, turned_ref, sems):
    copies = [pltpu.make_async_copy(source_ref.at[0], source_held.at[0], sems.at[0]),
              pltpu.make_async_copy(source_ref.at[1], source_held.at[1], sems.at[1]),
              pltpu.make_async_copy(kappa_ref, kappa_held, sems.at[2]),
              pltpu.make_async_copy(damping_ref, damping_held, sems.at[3])]
    for copy in copies:
        copy.start()
    odd, turn = path()
    for field in range(FIELDS):
        copies[field].wait()
        held = (source_held.at[0], source_held.at[1], kappa_held, damping_held)[field]
        for tile in range(CZ // LANES):
            here = slice(tile * LANES, (tile + 1) * LANES)
            turned_ref[field, here] = held[:, :, here].reshape(LANES, LANES).T
    for device in range(GROUP):
        rows = pl.ds(pl.multiple_of(slab_of(device, odd, turn) * SLAB, SLAB), SLAB)
        for field in range(FIELDS):
            out_ref[device, field] = turned_ref[field, rows]


def edges_kernel(got_ref, low_ref, high_ref):
    low_ref[...] = got_ref[:, :, 0:DEEP]
    high_ref[...] = got_ref[:, :, SLAB - DEEP:SLAB]


def total(values):
    return jnp.sum(jnp.sum(values, axis=0, keepdims=True), axis=1, keepdims=True)


def path():
    return lax.rem(lax.axis_index("sub") // GROUP, 2), lax.axis_index("shot")


def slab_of(device, odd, turn):
    half, y = (divmod(device, RING) if isinstance(device, int) else (device // RING, lax.rem(device, RING)))
    there = lax.rem(y - turn - 1 + 2 * RING, RING)
    back = RING + lax.rem(turn - y + 2 * RING, RING)
    return jnp.where(half == odd, there, back)


def device_of(slab, odd, turn):
    if slab < RING:
        return odd * RING + lax.rem(turn + 1 + slab, RING)
    return (1 - odd) * RING + lax.rem(turn - slab + 3 * RING, RING)


def position():
    odd, turn = path()
    place = slab_of(lax.rem(lax.axis_index("sub"), GROUP), odd, turn)
    return place == 0, place == GROUP - 1


class Steps:

    def __init__(self, u_ref, w_ref, d_ref):
        self.is_first, self.is_last = position()
        self.u_ref, self.w_ref, self.d_ref = u_ref, w_ref, d_ref
        for part in range(2):
            for plane in (0, PLANES - 1):
                u_ref[part, plane] = jnp.zeros((ROWS, LANES), jnp.float32)

    def swap_ends(self, ref):
        def run(a, b):
            for plane in range(2, 2 + CX):
                for part in range(2):
                    for at in tiles():
                        values = ref[part, plane, at]
                        lane = lax.rem(lanes_of(values), WIDE)
                        up = pltpu.roll(values, 3, 1)
                        down = pltpu.roll(values, LANES - 3, 1)
                        ref[part, plane, at] = jnp.where(lane == a, down, jnp.where(lane == b, up, values))

        @pl.when(self.is_first)
        def _():
            run(8, 10)

        @pl.when(self.is_last)
        def _():
            run(27, 29)

    def swap_sides(self, ref):
        one = jnp.zeros((TILE, LANES), jnp.float32)
        lane = lanes_of(one)
        last, first = CX + 1, 2

        def rows(slot):
            return slice(first_row(slot) + 1, first_row(slot) + 1 + CY)

        for part in range(2):
            for j in range(PY):
                here = rows(j)
                moved_up = pltpu.roll(ref[part, last, here], WIDE, 1)
                ref[part, 1, here] = jnp.where((lane >= WIDE) & (lane < 3 * WIDE), moved_up, ref[part, 1, here])
                slot, group = slot_of(PX - 1 + PX * j)
                end = rows(slot)
                inside = (lane >= group * WIDE) & (lane < (group + 1) * WIDE)
                shift = (2 - group) * WIDE
                moved_down = pltpu.roll(ref[part, first, here], LANES - WIDE, 1)
                from_end = pltpu.roll(ref[part, first, end], shift, 1) if shift else ref[part, first, end]
                ref[part, PLANES - 2, here] = jnp.where(
                    lane < 2 * WIDE, moved_down, jnp.where(lane < 3 * WIDE, from_end, ref[part, PLANES - 2, here]))
                to_end = ref[part, last, here]
                to_end = pltpu.roll(to_end, LANES - shift, 1) if shift else to_end
                ref[part, 1, end] = jnp.where(inside, to_end, ref[part, 1, end])

        def across(plane):
            for part in range(2):
                def row(slot, n):
                    return slice(first_row(slot) + n, first_row(slot) + n + 1)

                for j in range(PY):
                    if j > 0:
                        ref[part, plane, row(j, 0)] = ref[part, plane, row(j - 1, CY)]
                    if j < PY - 1:
                        ref[part, plane, row(j, CY + 1)] = ref[part, plane, row(j + 1, 1)]
                top = ref[part, plane, row(4, CY)]
                bottom = ref[part, plane, row(4, 1)]
                extra = ref[part, plane, row(5, 1)]
                lane = lanes_of(top)
                old = ref[part, plane, row(4, 0)]
                ref[part, plane, row(4, 0)] = jnp.where(
                    (lane >= WIDE) & (lane < 3 * WIDE), pltpu.roll(top, WIDE, 1), old)
                old = ref[part, plane, row(4, CY + 1)]
                ref[part, plane, row(4, CY + 1)] = jnp.where(
                    lane < 2 * WIDE, pltpu.roll(bottom, LANES - WIDE, 1),
                    jnp.where(lane < 3 * WIDE, pltpu.roll(extra, 2 * WIDE, 1), old))
                old = ref[part, plane, row(5, 0)]
                ref[part, plane, row(5, 0)] = jnp.where(lane < WIDE, pltpu.roll(top, LANES - 2 * WIDE, 1), old)

        for plane in range(1, PLANES - 1):
            across(plane)

    def mix(self, ref, plane):
        for part in range(2):
            for t in range(TILES):
                at = BASE + t * TILE
                here = ref[part, plane, at:at + TILE]
                mixed = ref[part, plane, at - 1:at + TILE - 1] + ref[part, plane, at + 1:at + TILE + 1] + MIDDLE * here
                self.u_ref[part, plane, at:at + TILE] = (
                    pltpu.roll(mixed, 1, 1) + pltpu.roll(mixed, LANES - 1, 1) + MIDDLE * mixed)

    def smoothed(self, part, plane, at):
        u_ref = self.u_ref
        return u_ref[part, plane - 1, at] + u_ref[part, plane + 1, at] + MIDDLE * u_ref[part, plane, at]

    def sweep(self, ref, first, last, body):
        for plane in range(1, first + 2):
            self.mix(ref, plane)
        for plane in range(first, last + 1):
            body(plane)
            if plane + 2 < PLANES - 1:
                self.mix(ref, plane + 2)

    def precondition(self, ref, right_ref):
        w_ref = self.w_ref
        for part in range(2):
            ref[part, :, 0:BASE] = jnp.zeros((PLANES, BASE, LANES), jnp.float32)
            ref[part, :, ROWS - 8:ROWS] = jnp.zeros((PLANES, 8, LANES), jnp.float32)

        def start(plane):
            for at in tiles():
                r_re, r_im = right_ref[0, plane, at], right_ref[1, plane, at]
                w_re, w_im = w_ref[0, plane, at], w_ref[1, plane, at]
                ref[0, plane, at] = w_re * r_re - w_im * r_im
                ref[1, plane, at] = w_re * r_im + w_im * r_re

        def update(plane):
            for at in tiles():
                z_re, z_im = ref[0, plane, at], ref[1, plane, at]
                w_re, w_im = w_ref[0, plane, at], w_ref[1, plane, at]
                g_re = (right_ref[0, plane, at] + self.smoothed(0, plane, at)) - PIVOT * z_re
                g_im = (right_ref[1, plane, at] + self.smoothed(1, plane, at)) - PIVOT * z_im
                ref[0, plane, at] = (1.0 - RELAX) * z_re + (w_re * g_re - w_im * g_im)
                ref[1, plane, at] = (1.0 - RELAX) * z_im + (w_re * g_im + w_im * g_re)

        for plane in range(1, PLANES - 1):
            start(plane)

        @pl.loop(0, SWEEPS - 1)
        def _(number):
            self.sweep(ref, 1, PLANES - 2, update)

        self.swap_ends(ref)
        self.swap_sides(ref)

    def image(self, ref, out_ref):
        d_ref = self.d_ref

        def body(plane):
            for at in tiles():
                z_re, z_im = ref[0, plane, at], ref[1, plane, at]
                d_re, d_im = d_ref[0, plane, at], d_ref[1, plane, at]
                out_ref[0, plane, at] = (d_re * z_re - d_im * z_im) - self.smoothed(0, plane, at)
                out_ref[1, plane, at] = (d_re * z_im + d_im * z_re) - self.smoothed(1, plane, at)

        self.sweep(ref, 2, PLANES - 3, body)


def tiles():
    return [slice(BASE + t * TILE, BASE + (t + 1) * TILE) for t in range(TILES)]


def send_back(ref, back_ref, first):
    for part in range(2):
        for slot in range(SLOTS):
            rows = slice(first_row(slot) + 1, first_row(slot) + 1 + CY)
            turned = ref[part, 2:2 + CX, rows].reshape(LANES, LANES).T
            for unit in range(GROUP):
                if slot_of(unit)[0] == slot:
                    at = slot_of(unit)[1] * WIDE + OWN
                    back_ref[unit, first + part * SLAB:first + (part + 1) * SLAB] = turned[at:at + SLAB]


def solve_kernel(got_ref, below_ref, above_ref, back_ref, r_ref, w_ref, d_ref, q_ref, z_ref, u_ref, turn_ref, turned_ref):
    is_first, is_last = position()
    low_at = jnp.where(is_first, 0, 3)
    high_at = jnp.where(is_last, 30, 27)

    turn_ref[...] = jnp.zeros_like(turn_ref)
    for ref in (r_ref, w_ref, d_ref):
        for plane in range(1, PLANES - 1):
            for part in range(2):
                ref[part, plane, BODY] = jnp.zeros((TILES * TILE, LANES), jnp.float32)
    for part in range(2):
        for plane in (1, PLANES - 2):
            q_ref[part, plane] = jnp.zeros((ROWS, LANES), jnp.float32)

    for unit in range(GROUP):
        slot, group = slot_of(unit)
        at = group * WIDE
        for field in range(FIELDS):
            turn_ref[slot, field, pl.ds(at + low_at, DEEP)] = below_ref[unit, field]
            turn_ref[slot, field, at + OWN:at + OWN + SLAB] = got_ref[unit, field]
            turn_ref[slot, field, pl.ds(at + high_at, DEEP)] = above_ref[unit, field]

    def fix(targets):
        for unit in range(GROUP):
            slot, group = slot_of(unit)
            at = group * WIDE
            for field in range(FIELDS):
                for target, ref, source in targets:
                    if ref is None:
                        row = jnp.zeros((1, LANES), jnp.float32)
                    else:
                        row = ref[unit, field, source:source + 1]
                    turn_ref[slot, field, at + target:at + target + 1] = row

    @pl.when(is_first)
    def _():
        fix(((8, got_ref, 0), (9, None, 0), (10, below_ref, DEEP - 1)))

    @pl.when(is_last)
    def _():
        fix(((27, above_ref, 0), (28, None, 0), (29, got_ref, SLAB - 1)))

    for slot in range(SLOTS):
        for field in range(FIELDS):
            turned_ref[slot, field] = turn_ref[slot, field].T

    def fill(plane, carry):
        at = pl.ds(pl.multiple_of(plane * TILE, TILE), TILE)
        for slot in range(SLOTS):
            b_re, b_im, kappa, damping = [turned_ref[slot, field, at] for field in range(FIELDS)]
            rows = slice(first_row(slot) + 1, first_row(slot) + 1 + CY)
            d_re = CENTER - kappa
            d_im = kappa * damping
            p_re = d_re - MIDDLE
            factor = jnp.where(kappa > 0, (RELAX / SCALE) / (p_re * p_re + d_im * d_im), 0.0)
            r_ref[0, 2 + plane, rows] = SCALE * b_re
            r_ref[1, 2 + plane, rows] = SCALE * b_im
            w_ref[0, 2 + plane, rows] = factor * p_re
            w_ref[1, 2 + plane, rows] = -factor * d_im
            d_ref[0, 2 + plane, rows] = SCALE * d_re
            d_ref[1, 2 + plane, rows] = SCALE * d_im
        return carry

    lax.fori_loop(0, CX, fill, 0, unroll=4)

    steps = Steps(u_ref, w_ref, d_ref)
    steps.swap_sides(r_ref)
    steps.swap_sides(w_ref)
    steps.precondition(z_ref, r_ref)
    send_back(z_ref, back_ref, 0)
    steps.image(z_ref, q_ref)
    steps.swap_ends(q_ref)
    steps.swap_sides(q_ref)
    steps.precondition(z_ref, q_ref)
    send_back(z_ref, back_ref, 2 * SLAB)
    steps.image(z_ref, w_ref)

    def own_cells(t):
        shape = (TILE, LANES)
        row = lax.broadcasted_iota(jnp.int32, shape, 0) + t * TILE
        lane = lax.broadcasted_iota(jnp.int32, shape, 1)
        y = lax.rem(row, SLOT)
        z = lax.rem(lane, WIDE)
        inside = (y >= 1) & (y <= CY) & (z >= OWN) & (z < OWN + SLAB)
        return inside & ((row < 5 * SLOT) & (lane < 3 * WIDE) | (row < SLOTS * SLOT) & (lane < WIDE))

    zero = jnp.zeros((TILE, LANES), jnp.float32)

    def first_sums(plane, sums):
        norm, proj_re, proj_im, cross_re, cross_im = sums
        for t, at in enumerate(tiles()):
            keep = own_cells(t)
            q_re = jnp.where(keep, q_ref[0, plane, at], 0.0)
            q_im = jnp.where(keep, q_ref[1, plane, at], 0.0)
            b_re, b_im = r_ref[0, plane, at], r_ref[1, plane, at]
            t_re, t_im = w_ref[0, plane, at], w_ref[1, plane, at]
            norm = norm + (q_re * q_re + q_im * q_im)
            proj_re = proj_re + (q_re * b_re + q_im * b_im)
            proj_im = proj_im + (q_re * b_im - q_im * b_re)
            cross_re = cross_re + (q_re * t_re + q_im * t_im)
            cross_im = cross_im + (q_re * t_im - q_im * t_re)
        return norm, proj_re, proj_im, cross_re, cross_im

    sums = (zero,) * 5
    for plane in range(2, 2 + CX):
        sums = first_sums(plane, sums)
    norm, proj_re, proj_im, cross_re, cross_im = [total(v) for v in sums]
    safe = jnp.where(norm > 0, norm, 1.0)
    cross_re = cross_re / safe
    cross_im = cross_im / safe

    def second_sums(plane, sums):
        rest, pair_re, pair_im = sums
        for t, at in enumerate(tiles()):
            keep = own_cells(t)
            q_re, q_im = q_ref[0, plane, at], q_ref[1, plane, at]
            b_re, b_im = r_ref[0, plane, at], r_ref[1, plane, at]
            p_re = jnp.where(keep, w_ref[0, plane, at] - (cross_re * q_re - cross_im * q_im), 0.0)
            p_im = jnp.where(keep, w_ref[1, plane, at] - (cross_re * q_im + cross_im * q_re), 0.0)
            rest = rest + (p_re * p_re + p_im * p_im)
            pair_re = pair_re + (p_re * b_re + p_im * b_im)
            pair_im = pair_im + (p_re * b_im - p_im * b_re)
        return rest, pair_re, pair_im

    sums = (zero,) * 3
    for plane in range(2, 2 + CX):
        sums = second_sums(plane, sums)
    rest, pair_re, pair_im = [total(v) for v in sums]
    row = lax.broadcasted_iota(jnp.int32, (STATS, LANES), 0)
    table = jnp.zeros((STATS, LANES), jnp.float32)
    for n, value in enumerate((norm, proj_re, proj_im, cross_re, cross_im, rest, pair_re, pair_im)):
        table = jnp.where(row == n, value, table)

    for unit in range(GROUP):
        back_ref[unit, FIELDS * SLAB:BACK] = table


def merged(rows):
    norm, proj_re, proj_im, cross_re, cross_im, rest, pair_re, pair_im = rows

    def over(values):
        return jnp.sum(values, axis=0, keepdims=True)

    whole = over(norm)
    mean_re = over(norm * cross_re) / whole
    mean_im = over(norm * cross_im) / whole
    off_re = cross_re - mean_re
    off_im = cross_im - mean_im
    return (whole, over(proj_re), over(proj_im), mean_re, mean_im,
            over(rest + norm * (off_re * off_re + off_im * off_im)),
            over(pair_re + off_re * proj_re + off_im * proj_im),
            over(pair_im + off_re * proj_im - off_im * proj_re))


def merge_kernel(back_ref, out_ref):
    rows = [back_ref[:, FIELDS * SLAB + n] for n in range(STATS)]
    for n, value in enumerate(merged(rows)):
        for target in range(PZ):
            out_ref[target, n:n + 1] = value


def finish_kernel(table_ref, back_ref, wave_ref, damping_ref, solution_ref, shares_ref):
    norm, proj_re, proj_im, mean_re, mean_im, size, pair_re, pair_im = merged([table_ref[:, n] for n in range(STATS)])
    beta_re = pair_re / size
    beta_im = pair_im / size
    lead_re = proj_re / norm - (beta_re * mean_re - beta_im * mean_im)
    lead_im = proj_im / norm - (beta_re * mean_im + beta_im * mean_re)
    shape = (SLAB, LANES)
    beta_re, beta_im, lead_re, lead_im = [jnp.broadcast_to(v, shape) for v in (beta_re, beta_im, lead_re, lead_im)]
    per = LANES // SLAB
    odd, turn = path()
    for tile in range(CZ // LANES):
        pieces = [[], []]
        for source in range(tile * per, (tile + 1) * per):
            at = device_of(source, odd, turn)
            f_re, f_im, s_re, s_im = [back_ref[at, n * SLAB:(n + 1) * SLAB] for n in range(FIELDS)]
            pieces[0].append((lead_re * f_re - lead_im * f_im) + (beta_re * s_re - beta_im * s_im))
            pieces[1].append((lead_re * f_im + lead_im * f_re) + (beta_re * s_im + beta_im * s_re))
        here = slice(tile * LANES, (tile + 1) * LANES)
        x_re, x_im = [jnp.concatenate(p, axis=0).T.reshape(CX, CY, LANES) for p in pieces]
        solution_ref[0, :, :, here] = x_re
        solution_ref[1, :, :, here] = x_im
        u_re, u_im = wave_ref[0, :, :, here], wave_ref[1, :, :, here]
        shares_ref[:, :, here] = (u_re * x_re + u_im * x_im) - damping_ref[:, :, here] * (u_im * x_re - u_re * x_im)


def moved(values, step):
    shots = lax.axis_size("shot")
    pairs = []
    for turn in range(shots):
        chain = []
        for layer in range(PZ):
            odd = layer % 2
            for slab in range(GROUP):
                if slab < RING:
                    device = odd * RING + (turn + 1 + slab) % RING
                else:
                    device = (1 - odd) * RING + (turn - slab) % RING
                chain.append((layer * GROUP + device) * shots + turn)
        pairs += list(zip(chain, chain[1:]) if step > 0 else zip(chain[1:], chain))
    return lax.ppermute(values, ("sub", "shot"), pairs)


def call(kernel, out_shapes, scratch=(), space=pltpu.VMEM, limit=VMEM_LIMIT):
    one = pl.BlockSpec(memory_space=pltpu.VMEM)
    given = pl.BlockSpec(memory_space=space)

    def run(*args):
        return pl.pallas_call(
            kernel,
            out_shape=[jax.ShapeDtypeStruct(shape, jnp.float32) for shape in out_shapes],
            in_specs=[given] * len(args),
            out_specs=[one] * len(out_shapes),
            scratch_shapes=list(scratch),
            compiler_params=pltpu.CompilerParams(vmem_limit_bytes=limit),
        )(*args)

    return run


def local(adjoint_source, forward_field, kappa, damping):
    source = adjoint_source[0, :, 0]
    wave = forward_field[0, :, 0]
    kappa = kappa[0]
    damping = damping[0]
    block = (CX, CY, CZ)
    held = [pltpu.VMEM(shape, jnp.float32) for shape in ((2,) + block, block, block, (FIELDS, CZ, LANES))]
    message, = call(turn_kernel, [(GROUP, FIELDS, SLAB, LANES)], held + [pltpu.SemaphoreType.DMA((FIELDS,))],
                    pltpu.HBM, 60 * 1024 * 1024)(source, kappa, damping)
    layers = [[k * GROUP + n for n in range(GROUP)] for k in range(PZ)]
    columns = [[k * GROUP + n for k in range(PZ)] for n in range(GROUP)]
    got = lax.all_to_all(message, "sub", 0, 0, axis_index_groups=layers)
    edge = (GROUP, FIELDS, DEEP, LANES)
    low, high = call(edges_kernel, [edge, edge])(got)
    below = moved(high, 1)
    above = moved(low, -1)
    work = pltpu.VMEM((2, PLANES, ROWS, LANES), jnp.float32)
    turn = pltpu.VMEM((SLOTS, FIELDS, LANES, LANES), jnp.float32)
    back, = call(solve_kernel, [(GROUP, BACK, LANES)], [work] * 6 + [turn] * 2)(got, below, above)
    back = lax.all_to_all(back, "sub", 0, 0, axis_index_groups=layers)
    part, = call(merge_kernel, [(PZ, STATS, LANES)])(back)
    table = lax.all_to_all(part, "sub", 0, 0, axis_index_groups=columns)
    solved, shares = call(finish_kernel, [(2, CX, CY, CZ), (CX, CY, CZ)])(table, back, wave, damping)
    shots = lax.axis_size("shot")
    shares = shares.reshape(shots, CX // shots, CY, CZ)
    share = jnp.sum(lax.all_to_all(shares, "shot", 0, 0), axis=0)
    return (solved[None, :, None], share[None])


def solution(mesh):
    return jax.shard_map(
        local,
        mesh=mesh,
        in_specs=(
            P("shot", None, "sub", None, None, None),
            P("shot", None, "sub", None, None, None),
            P("sub", None, None, None),
            P("sub", None, None, None),
        ),
        out_specs=(P("shot", None, "sub", None, None, None), P("sub", "shot", None, None)),
        check_vma=False,
    )
```

time: 126 us -> 115 us (0.913)
  Pallas kernels: 23.8 us -> 14.3 us
  local copies, waits for them, and re-layouts: 2.76 us -> 0.01 us
  blocking collectives: 89.6 us -> 87.9 us
    pallas_call x5, Pallas kernels: 23.8 us -> 14.3 us  [run(): pl.pallas_call(kernel, out_shape=[jax.ShapeDtypeStruct(shape, jnp.float32...]
    all_to_all x1, blocking collectives: 42.9 us -> 34.3 us  [local(): got = lax.all_to_all(message, 'sub', 0, 0, axis_index_groups=layers)]
    all_to_all x1, blocking collectives: 7.87 us -> 11.1 us  [local(): table = lax.all_to_all(part, 'sub', 0, 0, axis_index_groups=columns)]
    unnamed x10 -> x4, local copies, waits for them, and re-layouts: 2.76 us -> 0.01 us
    all_to_all x1, blocking collectives: 15.7 us -> 18 us  [local(): share = jnp.sum(lax.all_to_all(shares, 'shot', 0, 0), axis=0)]
    all_to_all x1, blocking collectives: 23.2 us -> 24.5 us  [local(): back = lax.all_to_all(back, 'sub', 0, 0, axis_index_groups=layers)]
  transfers between devices with their start and end apart: 2 -> 2, of which waited for: 1 -> 2; matrix products, arithmetic and copies ran while one was open for 0% -> 0% of each run, Pallas kernels for 0% -> 0%
where the time goes in v3:
time: 115 us; the launch traced here: 114 us
  blocking collectives  87.9 us (76%)
  Pallas kernels  14.3 us (12%)
  starting transfers between devices  6.49 us (6%)
  waiting for transfers between devices  4.42 us (4%)
    all_to_all x1, blocking collectives, local(): got = lax.all_to_all(message, 'sub', 0, 0, axis_index_groups=layers)  34.3 us
    all_to_all x1, blocking collectives, local(): back = lax.all_to_all(back, 'sub', 0, 0, axis_index_groups=layers)  24.5 us
    all_to_all x1, blocking collectives, local(): share = jnp.sum(lax.all_to_all(shares, 'shot', 0, 0), axis=0)  18 us
    pallas_call x5, Pallas kernels, run(): pl.pallas_call(kernel, out_shape=[jax.ShapeDtypeStruct(shape, jnp.float32...  14.3 us
    all_to_all x1, blocking collectives, local(): table = lax.all_to_all(part, 'sub', 0, 0, axis_index_groups=columns)  11.1 us
    ppermute x2, starting transfers between devices, moved(): return lax.ppermute(values, ('sub', 'shot'), pairs)  6.49 us
    ppermute x2, waiting for transfers between devices, moved(): return lax.ppermute(values, ('sub', 'shot'), pairs)  4.42 us
  transfers between devices with their start and end apart: 2, of which 2 were waited for; matrix products, arithmetic and copies ran while one was open for 0% of the time, Pallas kernels for 0%

profile of v3, /device:TPU:1, one launch (start us, length us, event | category | flops | bytes accessed | tf_op | source)
XLA Modules:
  0.0 114.4 jit_solution(6177013276739080077)
XLA Ops:
  0.6 2.2 %shard_map.59 = f32[16,4,16,128]{3,2,1,0:T(8,128)} custom-call(f32[2,16,8,256]{3,2,1,0:T(8,128)} %bitcast.13, f32[16,8,256]{2,1,0:T(8,128)} %bitcast.14, f32[16,8,256]{2,1,0:T(8,128)} %bitcast.9), custom_call_target="tpu_custom_call" | custom-call | tf_op jit(solution)/shard_map/pallas_call | solution.py:480
  2.8 34.3 %all_to_all.20.got_ref = f32[16,4,16,128]{3,2,1,0:T(8,128)S(1)} all-to-all(f32[16,4,16,128]{3,2,1,0:T(8,128)} %shard_map.59), channel_id=1, replica_groups={{0,8,16,24,32,40,48,56,64,72,80,88,96,104,112,120},{128,136,144,152,160..., dimensions={0} | all-to-all | bytes 1048576 | tf_op jit(solution)/shard_map/all_to_all | solution.py:503
  37.1 3.0 %collective-permute-start = (f32[16,4,8,128]{3,2,1,0:T(8,128)S(1)}, f32[16,4,8,128]{3,2,1,0:T(8,128)S(1)}, u32[]{:S(2)}, u32[]{:S(2)}) collective-permute-start(f32[16,4,8,128]{3,2,1,0:T(8,128)S(1)} %get-tuple-element.6), channel_id=1, source_target_pairs={{8,16},{16,24},{24,32},{32,40},{40,48},{48,56},{56,0},{0,64},{64,1... | collective-permute-start | bytes 786440 | tf_op jit(solution)/shard_map/ppermute | solution.py:472
  40.1 3.5 %collective-permute-start.1 = (f32[16,4,8,128]{3,2,1,0:T(8,128)S(1)}, f32[16,4,8,128]{3,2,1,0:T(8,128)S(1)}, u32[]{:S(2)}, u32[]{:S(2)}) collective-permute-start(f32[16,4,8,128]{3,2,1,0:T(8,128)S(1)} %get-tuple-element.7), channel_id=1, source_target_pairs={{16,8},{24,16},{32,24},{40,32},{48,40},{56,48},{0,56},{64,0},{120,... | collective-permute-start | bytes 786440 | tf_op jit(solution)/shard_map/ppermute | solution.py:472
  43.6 1.8 %collective-permute-done.below_ref = f32[16,4,8,128]{3,2,1,0:T(8,128)S(1)} collective-permute-done((f32[16,4,8,128]{3,2,1,0:T(8,128)S(1)}, f32[16,4,8,128]{3,2,1,0:T(8,128)S(1)}, u32[]{:S(2)}, u32[]{:S(2)}) %collective-permute-start) | collective-permute-done | bytes 262176 | tf_op jit(solution)/shard_map/ppermute | solution.py:472
  45.4 2.6 %collective-permute-done.1.above_ref = f32[16,4,8,128]{3,2,1,0:T(8,128)S(1)} collective-permute-done((f32[16,4,8,128]{3,2,1,0:T(8,128)S(1)}, f32[16,4,8,128]{3,2,1,0:T(8,128)S(1)}, u32[]{:S(2)}, u32[]{:S(2)}) %collective-permute-start.1) | collective-permute-done | bytes 262176 | tf_op jit(solution)/shard_map/ppermute | solution.py:472
  48.0 11.1 %shard_map.61 = f32[16,72,128]{2,1,0:T(8,128)S(1)} custom-call(f32[16,4,16,128]{3,2,1,0:T(8,128)S(1)} %all_to_all.20.got_ref, f32[16,4,8,128]{3,2,1,0:T(8,128)S(1)} %collective-permute-done.below_ref, f32[16,4,8,128]{3,2,1,0:T(8,128)S(1)} %collective-permute-done.1.above_ref), custom_call_target="tpu_custom_call" | custom-call | tf_op jit(solution)/shard_map/pallas_call | solution.py:480
  59.2 24.5 %all_to_all.21.back_ref = f32[16,72,128]{2,1,0:T(8,128)S(1)} all-to-all(f32[16,72,128]{2,1,0:T(8,128)S(1)} %shard_map.61), channel_id=1, replica_groups={{0,8,16,24,32,40,48,56,64,72,80,88,96,104,112,120},{128,136,144,152,160..., dimensions={0} | all-to-all | bytes 1179648 | tf_op jit(solution)/shard_map/all_to_all | solution.py:511
  83.7 0.0 copy-start
  83.7 0.0 copy-start.1
  83.7 0.1 shard_map.62
  83.8 11.1 %all_to_all.22.table_ref = f32[4,8,128]{2,1,0:T(8,128)S(1)} all-to-all(f32[4,8,128]{2,1,0:T(8,128)S(1)} %shard_map.62), channel_id=1, replica_groups={{0,128,256,384},{8,136,264,392},{16,144,272,400},{24,152,280,408},{32,1..., dimensions={0} | all-to-all | bytes 32768 | tf_op jit(solution)/shard_map/all_to_all | solution.py:513
  94.9 0.0 copy-done
  94.9 0.0 copy-done.1
  94.9 0.9 shard_map.63
  95.8 18.0 %all_to_all.23 = f32[8,2,8,256]{3,2,1,0:T(8,128)S(1)} all-to-all(f32[8,2,8,256]{3,2,1,0:T(8,128)S(1)} %bitcast.12), channel_id=1, replica_groups=mesh['sub'=64,'shot'=8] {'shot'}, dimensions={0} | all-to-all | bytes 262144 | tf_op jit(solution)/shard_map/all_to_all | solution.py:517
  113.7 0.6 reduce_sum.9
  (1 shorter events, 0.0 us)
Async XLA Ops:
  37.1 8.3 %collective-permute-start = (f32[16,4,8,128]{3,2,1,0:T(8,128)S(1)}, f32[16,4,8,128]{3,2,1,0:T(8,128)S(1)}, u32[]{:S(2)}, u32[]{:S(2)}) collective-permute-start(f32[16,4,8,128]{3,2,1,0:T(8,128)S(1)} %get-tuple-element.6), channel_id=1, source_target_pairs={{8,16},{16,24},{24,32},{32,40},{40,48},{48,56},{56,0},{0,64},{64,1... | collective-permute-start | bytes 786440 | tf_op jit(solution)/shard_map/ppermute | solution.py:472
  40.1 7.9 %collective-permute-start.1 = (f32[16,4,8,128]{3,2,1,0:T(8,128)S(1)}, f32[16,4,8,128]{3,2,1,0:T(8,128)S(1)}, u32[]{:S(2)}, u32[]{:S(2)}) collective-permute-start(f32[16,4,8,128]{3,2,1,0:T(8,128)S(1)} %get-tuple-element.7), channel_id=1, source_target_pairs={{16,8},{24,16},{32,24},{40,32},{48,40},{56,48},{0,56},{64,0},{120,... | collective-permute-start | bytes 786440 | tf_op jit(solution)/shard_map/ppermute | solution.py:472
  83.7 11.2 %copy-start = (f32[1,16,8,256]{3,2,1,0:T(8,128)S(1)}, f32[1,16,8,256]{3,2,1,0:T(8,128)}, u32[]{:S(2)}) copy-start(f32[1,16,8,256]{3,2,1,0:T(8,128)} %param.7) | copy-start | bytes 393220
  83.7 11.2 %copy-start.1 = (f32[1,2,1,16,8,256]{5,4,3,2,1,0:T(8,128)S(1)}, f32[1,2,1,16,8,256]{5,4,3,2,1,0:T(8,128)}, u32[]{:S(2)}) copy-start(f32[1,2,1,16,8,256]{5,4,3,2,1,0:T(8,128)} %param.5) | copy-start | bytes 786436

commit v4 on v3

--- a/solution.py
+++ b/solution.py
@@ -119,14 +119,14 @@
 
     def swap_ends(self, ref):
         def run(a, b):
+            lane = lax.broadcasted_iota(jnp.int32, (TILE, LANES), 1)
+            place = lax.rem(lane, WIDE)
+            source = jnp.where(place == a, lane + 3, jnp.where(place == b, lane - 3, lane))
+            source = jnp.minimum(source, LANES - 1)
             for plane in range(2, 2 + CX):
                 for part in range(2):
-                    for at in tiles():
-                        values = ref[part, plane, at]
-                        lane = lax.rem(lanes_of(values), WIDE)
-                        up = pltpu.roll(values, 3, 1)
-                        down = pltpu.roll(values, LANES - 3, 1)
-                        ref[part, plane, at] = jnp.where(lane == a, down, jnp.where(lane == b, up, values))
+                    for at in own_tiles():
+                        ref[part, plane, at] = jnp.take_along_axis(ref[part, plane, at], source, axis=1)
 
         @pl.when(self.is_first)
         def _():
@@ -188,26 +188,25 @@
         for plane in range(1, PLANES - 1):
             across(plane)
 
-    def mix(self, ref, plane):
+    def mix(self, ref, plane, rows):
         for part in range(2):
-            for t in range(TILES):
-                at = BASE + t * TILE
-                here = ref[part, plane, at:at + TILE]
-                mixed = ref[part, plane, at - 1:at + TILE - 1] + ref[part, plane, at + 1:at + TILE + 1] + MIDDLE * here
-                self.u_ref[part, plane, at:at + TILE] = (
+            for at in rows:
+                below, above = slice(at.start - 1, at.stop - 1), slice(at.start + 1, at.stop + 1)
+                mixed = ref[part, plane, below] + ref[part, plane, above] + MIDDLE * ref[part, plane, at]
+                self.u_ref[part, plane, at] = (
                     pltpu.roll(mixed, 1, 1) + pltpu.roll(mixed, LANES - 1, 1) + MIDDLE * mixed)
 
     def smoothed(self, part, plane, at):
         u_ref = self.u_ref
         return u_ref[part, plane - 1, at] + u_ref[part, plane + 1, at] + MIDDLE * u_ref[part, plane, at]
 
-    def sweep(self, ref, first, last, body):
+    def sweep(self, ref, first, last, body, rows):
         for plane in range(1, first + 2):
-            self.mix(ref, plane)
+            self.mix(ref, plane, rows)
         for plane in range(first, last + 1):
-            body(plane)
+            body(plane, rows)
             if plane + 2 < PLANES - 1:
-                self.mix(ref, plane + 2)
+                self.mix(ref, plane + 2, rows)
 
     def precondition(self, ref, right_ref):
         w_ref = self.w_ref
@@ -222,8 +221,8 @@
                 ref[0, plane, at] = w_re * r_re - w_im * r_im
                 ref[1, plane, at] = w_re * r_im + w_im * r_re
 
-        def update(plane):
-            for at in tiles():
+        def update(plane, rows):
+            for at in rows:
                 z_re, z_im = ref[0, plane, at], ref[1, plane, at]
                 w_re, w_im = w_ref[0, plane, at], w_ref[1, plane, at]
                 g_re = (right_ref[0, plane, at] + self.smoothed(0, plane, at)) - PIVOT * z_re
@@ -234,28 +233,33 @@
         for plane in range(1, PLANES - 1):
             start(plane)
 
-        @pl.loop(0, SWEEPS - 1)
+        @pl.loop(0, SWEEPS - 2)
         def _(number):
-            self.sweep(ref, 1, PLANES - 2, update)
-
+            self.sweep(ref, 1, PLANES - 2, update, tiles())
+
+        self.sweep(ref, 2, PLANES - 3, update, own_tiles())
         self.swap_ends(ref)
         self.swap_sides(ref)
 
     def image(self, ref, out_ref):
         d_ref = self.d_ref
 
-        def body(plane):
-            for at in tiles():
+        def body(plane, rows):
+            for at in rows:
                 z_re, z_im = ref[0, plane, at], ref[1, plane, at]
                 d_re, d_im = d_ref[0, plane, at], d_ref[1, plane, at]
                 out_ref[0, plane, at] = (d_re * z_re - d_im * z_im) - self.smoothed(0, plane, at)
                 out_ref[1, plane, at] = (d_re * z_im + d_im * z_re) - self.smoothed(1, plane, at)
 
-        self.sweep(ref, 2, PLANES - 3, body)
+        self.sweep(ref, 2, PLANES - 3, body, own_tiles())
 
 
 def tiles():
     return [slice(BASE + t * TILE, BASE + (t + 1) * TILE) for t in range(TILES)]
+
+
+def own_tiles():
+    return [slice(first_row(slot) + 1, first_row(slot) + 1 + CY) for slot in range(SLOTS)]
 
 
 def send_back(ref, back_ref, first):
@@ -275,13 +279,10 @@
     high_at = jnp.where(is_last, 30, 27)
 
     turn_ref[...] = jnp.zeros_like(turn_ref)
-    for ref in (r_ref, w_ref, d_ref):
+    for ref in (r_ref, w_ref, d_ref, q_ref):
         for plane in range(1, PLANES - 1):
             for part in range(2):
                 ref[part, plane, BODY] = jnp.zeros((TILES * TILE, LANES), jnp.float32)
-    for part in range(2):
-        for plane in (1, PLANES - 2):
-            q_ref[part, plane] = jnp.zeros((ROWS, LANES), jnp.float32)
 
     for unit in range(GROUP):
         slot, group = slot_of(unit)
@@ -346,57 +347,42 @@
     send_back(z_ref, back_ref, 2 * SLAB)
     steps.image(z_ref, w_ref)
 
-    def own_cells(t):
-        shape = (TILE, LANES)
-        row = lax.broadcasted_iota(jnp.int32, shape, 0) + t * TILE
-        lane = lax.broadcasted_iota(jnp.int32, shape, 1)
-        y = lax.rem(row, SLOT)
-        z = lax.rem(lane, WIDE)
-        inside = (y >= 1) & (y <= CY) & (z >= OWN) & (z < OWN + SLAB)
-        return inside & ((row < 5 * SLOT) & (lane < 3 * WIDE) | (row < SLOTS * SLOT) & (lane < WIDE))
-
-    zero = jnp.zeros((TILE, LANES), jnp.float32)
-
-    def first_sums(plane, sums):
-        norm, proj_re, proj_im, cross_re, cross_im = sums
-        for t, at in enumerate(tiles()):
-            keep = own_cells(t)
-            q_re = jnp.where(keep, q_ref[0, plane, at], 0.0)
-            q_im = jnp.where(keep, q_ref[1, plane, at], 0.0)
-            b_re, b_im = r_ref[0, plane, at], r_ref[1, plane, at]
-            t_re, t_im = w_ref[0, plane, at], w_ref[1, plane, at]
-            norm = norm + (q_re * q_re + q_im * q_im)
-            proj_re = proj_re + (q_re * b_re + q_im * b_im)
-            proj_im = proj_im + (q_re * b_im - q_im * b_re)
-            cross_re = cross_re + (q_re * t_re + q_im * t_im)
-            cross_im = cross_im + (q_re * t_im - q_im * t_re)
-        return norm, proj_re, proj_im, cross_re, cross_im
-
-    sums = (zero,) * 5
-    for plane in range(2, 2 + CX):
-        sums = first_sums(plane, sums)
-    norm, proj_re, proj_im, cross_re, cross_im = [total(v) for v in sums]
+    lane = lax.broadcasted_iota(jnp.int32, (TILE, LANES), 1)
+    place = lax.rem(lane, WIDE)
+    in_slab = (place >= OWN) & (place < OWN + SLAB)
+
+    def over_cells(terms, count):
+        sums = [jnp.zeros((TILE, LANES), jnp.float32)] * count
+        for slot, at in enumerate(own_tiles()):
+            here = terms(2, at)
+            for plane in range(3, 2 + CX):
+                here = [a + b for a, b in zip(here, terms(plane, at))]
+            keep = in_slab if slot < SLOTS - 1 else in_slab & (lane < WIDE)
+            sums = [a + jnp.where(keep, b, 0.0) for a, b in zip(sums, here)]
+        return [total(v) for v in sums]
+
+    def first_terms(plane, at):
+        q_re, q_im = q_ref[0, plane, at], q_ref[1, plane, at]
+        b_re, b_im = r_ref[0, plane, at], r_ref[1, plane, at]
+        t_re, t_im = w_ref[0, plane, at], w_ref[1, plane, at]
+        return (q_re * q_re + q_im * q_im, q_re * b_re + q_im * b_im, q_re * b_im - q_im * b_re,
+                q_re * t_re + q_im * t_im, q_re * t_im - q_im * t_re)
+
+    norm, proj_re, proj_im, cross_re, cross_im = over_cells(first_terms, 5)
     safe = jnp.where(norm > 0, norm, 1.0)
     cross_re = cross_re / safe
     cross_im = cross_im / safe
-
-    def second_sums(plane, sums):
-        rest, pair_re, pair_im = sums
-        for t, at in enumerate(tiles()):
-            keep = own_cells(t)
-            q_re, q_im = q_ref[0, plane, at], q_ref[1, plane, at]
-            b_re, b_im = r_ref[0, plane, at], r_ref[1, plane, at]
-            p_re = jnp.where(keep, w_ref[0, plane, at] - (cross_re * q_re - cross_im * q_im), 0.0)
-            p_im = jnp.where(keep, w_ref[1, plane, at] - (cross_re * q_im + cross_im * q_re), 0.0)
-            rest = rest + (p_re * p_re + p_im * p_im)
-            pair_re = pair_re + (p_re * b_re + p_im * b_im)
-            pair_im = pair_im + (p_re * b_im - p_im * b_re)
-        return rest, pair_re, pair_im
-
-    sums = (zero,) * 3
-    for plane in range(2, 2 + CX):
-        sums = second_sums(plane, sums)
-    rest, pair_re, pair_im = [total(v) for v in sums]
+    mean_re = jnp.broadcast_to(cross_re, (TILE, LANES))
+    mean_im = jnp.broadcast_to(cross_im, (TILE, LANES))
+
+    def second_terms(plane, at):
+        q_re, q_im = q_ref[0, plane, at], q_ref[1, plane, at]
+        b_re, b_im = r_ref[0, plane, at], r_ref[1, plane, at]
+        p_re = w_ref[0, plane, at] - (mean_re * q_re - mean_im * q_im)
+        p_im = w_ref[1, plane, at] - (mean_re * q_im + mean_im * q_re)
+        return p_re * p_re + p_im * p_im, p_re * b_re + p_im * b_im, p_re * b_im - p_im * b_re
+
+    rest, pair_re, pair_im = over_cells(second_terms, 3)
     row = lax.broadcasted_iota(jnp.int32, (STATS, LANES), 0)
     table = jnp.zeros((STATS, LANES), jnp.float32)
     for n, value in enumerate((norm, proj_re, proj_im, cross_re, cross_im, rest, pair_re, pair_im)):

time: 115 us -> 113 us (0.983)
  Pallas kernels: 14.3 us -> 12.9 us
    pallas_call x5, Pallas kernels: 14.3 us -> 12.9 us  [run(): pl.pallas_call(kernel, out_shape=[jax.ShapeDtypeStruct(shape, jnp.float32...]
where the time goes in v4:
time: 113 us
  blocking collectives  87.9 us (78%)
  Pallas kernels  12.9 us (11%)
  starting transfers between devices  6.49 us (6%)
  waiting for transfers between devices  4.42 us (4%)
    all_to_all x1, blocking collectives, local(): got = lax.all_to_all(message, 'sub', 0, 0, axis_index_groups=layers)  34.3 us
    all_to_all x1, blocking collectives, local(): back = lax.all_to_all(back, 'sub', 0, 0, axis_index_groups=layers)  24.5 us
    all_to_all x1, blocking collectives, local(): share = jnp.sum(lax.all_to_all(shares, 'shot', 0, 0), axis=0)  18 us
    pallas_call x5, Pallas kernels, run(): pl.pallas_call(kernel, out_shape=[jax.ShapeDtypeStruct(shape, jnp.float32...  12.9 us
    all_to_all x1, blocking collectives, local(): table = lax.all_to_all(part, 'sub', 0, 0, axis_index_groups=columns)  11.1 us
    ppermute x2, starting transfers between devices, moved(): return lax.ppermute(values, ('sub', 'shot'), pairs)  6.49 us
    ppermute x2, waiting for transfers between devices, moved(): return lax.ppermute(values, ('sub', 'shot'), pairs)  4.42 us
  transfers between devices with their start and end apart: 2, of which 2 were waited for; matrix products, arithmetic and copies ran while one was open for 0% of the time, Pallas kernels for 0%

profile of v4, /device:TPU:1, one launch (start us, length us, event | category | flops | bytes accessed | tf_op | source)
XLA Modules:
  0.0 113.0 jit_solution(384698935928524009)
XLA Ops:
  0.6 2.2 %shard_map.59 = f32[16,4,16,128]{3,2,1,0:T(8,128)} custom-call(f32[2,16,8,256]{3,2,1,0:T(8,128)} %bitcast.13, f32[16,8,256]{2,1,0:T(8,128)} %bitcast.14, f32[16,8,256]{2,1,0:T(8,128)} %bitcast.9), custom_call_target="tpu_custom_call" | custom-call | tf_op jit(solution)/shard_map/pallas_call | solution.py:466
  2.8 34.3 %all_to_all.20.got_ref = f32[16,4,16,128]{3,2,1,0:T(8,128)S(1)} all-to-all(f32[16,4,16,128]{3,2,1,0:T(8,128)} %shard_map.59), channel_id=1, replica_groups={{0,8,16,24,32,40,48,56,64,72,80,88,96,104,112,120},{128,136,144,152,160..., dimensions={0} | all-to-all | bytes 1048576 | tf_op jit(solution)/shard_map/all_to_all | solution.py:489
  37.1 3.0 %collective-permute-start = (f32[16,4,8,128]{3,2,1,0:T(8,128)S(1)}, f32[16,4,8,128]{3,2,1,0:T(8,128)S(1)}, u32[]{:S(2)}, u32[]{:S(2)}) collective-permute-start(f32[16,4,8,128]{3,2,1,0:T(8,128)S(1)} %get-tuple-element.6), channel_id=1, source_target_pairs={{8,16},{16,24},{24,32},{32,40},{40,48},{48,56},{56,0},{0,64},{64,1... | collective-permute-start | bytes 786440 | tf_op jit(solution)/shard_map/ppermute | solution.py:458
  40.1 3.5 %collective-permute-start.1 = (f32[16,4,8,128]{3,2,1,0:T(8,128)S(1)}, f32[16,4,8,128]{3,2,1,0:T(8,128)S(1)}, u32[]{:S(2)}, u32[]{:S(2)}) collective-permute-start(f32[16,4,8,128]{3,2,1,0:T(8,128)S(1)} %get-tuple-element.7), channel_id=1, source_target_pairs={{16,8},{24,16},{32,24},{40,32},{48,40},{56,48},{0,56},{64,0},{120,... | collective-permute-start | bytes 786440 | tf_op jit(solution)/shard_map/ppermute | solution.py:458
  43.6 1.8 %collective-permute-done.below_ref = f32[16,4,8,128]{3,2,1,0:T(8,128)S(1)} collective-permute-done((f32[16,4,8,128]{3,2,1,0:T(8,128)S(1)}, f32[16,4,8,128]{3,2,1,0:T(8,128)S(1)}, u32[]{:S(2)}, u32[]{:S(2)}) %collective-permute-start) | collective-permute-done | bytes 262176 | tf_op jit(solution)/shard_map/ppermute | solution.py:458
  45.4 2.6 %collective-permute-done.1.above_ref = f32[16,4,8,128]{3,2,1,0:T(8,128)S(1)} collective-permute-done((f32[16,4,8,128]{3,2,1,0:T(8,128)S(1)}, f32[16,4,8,128]{3,2,1,0:T(8,128)S(1)}, u32[]{:S(2)}, u32[]{:S(2)}) %collective-permute-start.1) | collective-permute-done | bytes 262176 | tf_op jit(solution)/shard_map/ppermute | solution.py:458
  48.0 9.7 %shard_map.61 = f32[16,72,128]{2,1,0:T(8,128)S(1)} custom-call(f32[16,4,16,128]{3,2,1,0:T(8,128)S(1)} %all_to_all.20.got_ref, f32[16,4,8,128]{3,2,1,0:T(8,128)S(1)} %collective-permute-done.below_ref, f32[16,4,8,128]{3,2,1,0:T(8,128)S(1)} %collective-permute-done.1.above_ref), custom_call_target="tpu_custom_call" | custom-call | tf_op jit(solution)/shard_map/pallas_call | solution.py:466
  57.8 24.5 %all_to_all.21.back_ref = f32[16,72,128]{2,1,0:T(8,128)S(1)} all-to-all(f32[16,72,128]{2,1,0:T(8,128)S(1)} %shard_map.61), channel_id=1, replica_groups={{0,8,16,24,32,40,48,56,64,72,80,88,96,104,112,120},{128,136,144,152,160..., dimensions={0} | all-to-all | bytes 1179648 | tf_op jit(solution)/shard_map/all_to_all | solution.py:497
  82.3 0.0 copy-start
  82.3 0.0 copy-start.1
  82.3 0.1 shard_map.62
  82.4 11.1 %all_to_all.22.table_ref = f32[4,8,128]{2,1,0:T(8,128)S(1)} all-to-all(f32[4,8,128]{2,1,0:T(8,128)S(1)} %shard_map.62), channel_id=1, replica_groups={{0,128,256,384},{8,136,264,392},{16,144,272,400},{24,152,280,408},{32,1..., dimensions={0} | all-to-all | bytes 32768 | tf_op jit(solution)/shard_map/all_to_all | solution.py:499
  93.5 0.0 copy-done
  93.5 0.0 copy-done.1
  93.5 0.9 shard_map.63
  94.4 18.0 %all_to_all.23 = f32[8,2,8,256]{3,2,1,0:T(8,128)S(1)} all-to-all(f32[8,2,8,256]{3,2,1,0:T(8,128)S(1)} %bitcast.12), channel_id=1, replica_groups=mesh['sub'=64,'shot'=8] {'shot'}, dimensions={0} | all-to-all | bytes 262144 | tf_op jit(solution)/shard_map/all_to_all | solution.py:503
  112.3 0.6 reduce_sum.9
  (1 shorter events, 0.0 us)
Async XLA Ops:
  37.1 8.3 %collective-permute-start = (f32[16,4,8,128]{3,2,1,0:T(8,128)S(1)}, f32[16,4,8,128]{3,2,1,0:T(8,128)S(1)}, u32[]{:S(2)}, u32[]{:S(2)}) collective-permute-start(f32[16,4,8,128]{3,2,1,0:T(8,128)S(1)} %get-tuple-element.6), channel_id=1, source_target_pairs={{8,16},{16,24},{24,32},{32,40},{40,48},{48,56},{56,0},{0,64},{64,1... | collective-permute-start | bytes 786440 | tf_op jit(solution)/shard_map/ppermute | solution.py:458
  40.1 7.9 %collective-permute-start.1 = (f32[16,4,8,128]{3,2,1,0:T(8,128)S(1)}, f32[16,4,8,128]{3,2,1,0:T(8,128)S(1)}, u32[]{:S(2)}, u32[]{:S(2)}) collective-permute-start(f32[16,4,8,128]{3,2,1,0:T(8,128)S(1)} %get-tuple-element.7), channel_id=1, source_target_pairs={{16,8},{24,16},{32,24},{40,32},{48,40},{56,48},{0,56},{64,0},{120,... | collective-permute-start | bytes 786440 | tf_op jit(solution)/shard_map/ppermute | solution.py:458
  82.3 11.2 %copy-start = (f32[1,16,8,256]{3,2,1,0:T(8,128)S(1)}, f32[1,16,8,256]{3,2,1,0:T(8,128)}, u32[]{:S(2)}) copy-start(f32[1,16,8,256]{3,2,1,0:T(8,128)} %param.7) | copy-start | bytes 393220
  82.3 11.2 %copy-start.1 = (f32[1,2,1,16,8,256]{5,4,3,2,1,0:T(8,128)S(1)}, f32[1,2,1,16,8,256]{5,4,3,2,1,0:T(8,128)}, u32[]{:S(2)}) copy-start(f32[1,2,1,16,8,256]{5,4,3,2,1,0:T(8,128)} %param.5) | copy-start | bytes 786436

commit v5 on v4

--- a/solution.py
+++ b/solution.py
@@ -273,7 +273,7 @@
                     back_ref[unit, first + part * SLAB:first + (part + 1) * SLAB] = turned[at:at + SLAB]
 
 
-def solve_kernel(got_ref, below_ref, above_ref, back_ref, r_ref, w_ref, d_ref, q_ref, z_ref, u_ref, turn_ref, turned_ref):
+def solve_kernel(got_ref, below_ref, above_ref, back_ref, sums_ref, r_ref, w_ref, d_ref, q_ref, z_ref, u_ref, turn_ref, turned_ref):
     is_first, is_last = position()
     low_at = jnp.where(is_first, 0, 3)
     high_at = jnp.where(is_last, 30, 27)
@@ -388,8 +388,8 @@
     for n, value in enumerate((norm, proj_re, proj_im, cross_re, cross_im, rest, pair_re, pair_im)):
         table = jnp.where(row == n, value, table)
 
-    for unit in range(GROUP):
-        back_ref[unit, FIELDS * SLAB:BACK] = table
+    for target in range(PZ):
+        sums_ref[target] = table
 
 
 def merged(rows):
@@ -409,15 +409,17 @@
             over(pair_im + off_re * proj_im - off_im * proj_re))
 
 
-def merge_kernel(back_ref, out_ref):
+def pack_kernel(table_ref, back_ref, out_ref):
+    for n, value in enumerate(merged([table_ref[:, n] for n in range(STATS)])):
+        for unit in range(GROUP):
+            out_ref[unit, FIELDS * SLAB + n:FIELDS * SLAB + n + 1] = value
+    for unit in range(GROUP):
+        out_ref[unit, 0:FIELDS * SLAB] = back_ref[unit]
+
+
+def finish_kernel(back_ref, wave_ref, damping_ref, solution_ref, shares_ref):
     rows = [back_ref[:, FIELDS * SLAB + n] for n in range(STATS)]
-    for n, value in enumerate(merged(rows)):
-        for target in range(PZ):
-            out_ref[target, n:n + 1] = value
-
-
-def finish_kernel(table_ref, back_ref, wave_ref, damping_ref, solution_ref, shares_ref):
-    norm, proj_re, proj_im, mean_re, mean_im, size, pair_re, pair_im = merged([table_ref[:, n] for n in range(STATS)])
+    norm, proj_re, proj_im, mean_re, mean_im, size, pair_re, pair_im = merged(rows)
     beta_re = pair_re / size
     beta_im = pair_im / size
     lead_re = proj_re / norm - (beta_re * mean_re - beta_im * mean_im)
@@ -493,11 +495,12 @@
     above = moved(low, -1)
     work = pltpu.VMEM((2, PLANES, ROWS, LANES), jnp.float32)
     turn = pltpu.VMEM((SLOTS, FIELDS, LANES, LANES), jnp.float32)
-    back, = call(solve_kernel, [(GROUP, BACK, LANES)], [work] * 6 + [turn] * 2)(got, below, above)
+    back, sums = call(solve_kernel, [(GROUP, FIELDS * SLAB, LANES), (PZ, STATS, LANES)],
+                      [work] * 6 + [turn] * 2)(got, below, above)
+    table = lax.all_to_all(sums, "sub", 0, 0, axis_index_groups=columns)
+    back, = call(pack_kernel, [(GROUP, BACK, LANES)])(table, back)
     back = lax.all_to_all(back, "sub", 0, 0, axis_index_groups=layers)
-    part, = call(merge_kernel, [(PZ, STATS, LANES)])(back)
-    table = lax.all_to_all(part, "sub", 0, 0, axis_index_groups=columns)
-    solved, shares = call(finish_kernel, [(2, CX, CY, CZ), (CX, CY, CZ)])(table, back, wave, damping)
+    solved, shares = call(finish_kernel, [(2, CX, CY, CZ), (CX, CY, CZ)])(back, wave, damping)
     shots = lax.axis_size("shot")
     shares = shares.reshape(shots, CX // shots, CY, CZ)
     share = jnp.sum(lax.all_to_all(shares, "shot", 0, 0), axis=0)

time: 113 us -> 112 us (level)
  blocking collectives: 87.9 us -> 86.2 us
    all_to_all x1, blocking collectives: 11.1 us -> 9.53 us  [local(): table = lax.all_to_all(sums, 'sub', 0, 0, axis_index_groups=columns)]
where the time goes in v5:
time: 112 us; the launch traced here: 111 us
  blocking collectives  86.2 us (77%)
  Pallas kernels  12.9 us (12%)
  starting transfers between devices  6.49 us (6%)
  waiting for transfers between devices  4.42 us (4%)
    all_to_all x1, blocking collectives, local(): got = lax.all_to_all(message, 'sub', 0, 0, axis_index_groups=layers)  34.3 us
    all_to_all x1, blocking collectives, local(): back = lax.all_to_all(back, 'sub', 0, 0, axis_index_groups=layers)  24.7 us
    all_to_all x1, blocking collectives, local(): share = jnp.sum(lax.all_to_all(shares, 'shot', 0, 0), axis=0)  17.7 us
    pallas_call x5, Pallas kernels, run(): pl.pallas_call(kernel, out_shape=[jax.ShapeDtypeStruct(shape, jnp.float32...  12.9 us
    all_to_all x1, blocking collectives, local(): table = lax.all_to_all(sums, 'sub', 0, 0, axis_index_groups=columns)  9.53 us
    ppermute x2, starting transfers between devices, moved(): return lax.ppermute(values, ('sub', 'shot'), pairs)  6.49 us
    ppermute x2, waiting for transfers between devices, moved(): return lax.ppermute(values, ('sub', 'shot'), pairs)  4.42 us
  transfers between devices with their start and end apart: 2, of which 2 were waited for; matrix products, arithmetic and copies ran while one was open for 0% of the time, Pallas kernels for 0%

profile of v5, /device:TPU:1, one launch (start us, length us, event | category | flops | bytes accessed | tf_op | source)
XLA Modules:
  0.0 111.4 jit_solution(7434431269872614952)
XLA Ops:
  0.6 2.2 %shard_map.59 = f32[16,4,16,128]{3,2,1,0:T(8,128)} custom-call(f32[2,16,8,256]{3,2,1,0:T(8,128)} %bitcast.13, f32[16,8,256]{2,1,0:T(8,128)} %bitcast.14, f32[16,8,256]{2,1,0:T(8,128)} %bitcast.9), custom_call_target="tpu_custom_call" | custom-call | tf_op jit(solution)/shard_map/pallas_call | solution.py:468
  2.8 34.3 %all_to_all.20.got_ref = f32[16,4,16,128]{3,2,1,0:T(8,128)S(1)} all-to-all(f32[16,4,16,128]{3,2,1,0:T(8,128)} %shard_map.59), channel_id=1, replica_groups={{0,8,16,24,32,40,48,56,64,72,80,88,96,104,112,120},{128,136,144,152,160..., dimensions={0} | all-to-all | bytes 1048576 | tf_op jit(solution)/shard_map/all_to_all | solution.py:491
  37.1 3.0 %collective-permute-start = (f32[16,4,8,128]{3,2,1,0:T(8,128)S(1)}, f32[16,4,8,128]{3,2,1,0:T(8,128)S(1)}, u32[]{:S(2)}, u32[]{:S(2)}) collective-permute-start(f32[16,4,8,128]{3,2,1,0:T(8,128)S(1)} %get-tuple-element.8), channel_id=1, source_target_pairs={{8,16},{16,24},{24,32},{32,40},{40,48},{48,56},{56,0},{0,64},{64,1... | collective-permute-start | bytes 786440 | tf_op jit(solution)/shard_map/ppermute | solution.py:460
  40.1 3.5 %collective-permute-start.1 = (f32[16,4,8,128]{3,2,1,0:T(8,128)S(1)}, f32[16,4,8,128]{3,2,1,0:T(8,128)S(1)}, u32[]{:S(2)}, u32[]{:S(2)}) collective-permute-start(f32[16,4,8,128]{3,2,1,0:T(8,128)S(1)} %get-tuple-element.9), channel_id=1, source_target_pairs={{16,8},{24,16},{32,24},{40,32},{48,40},{56,48},{0,56},{64,0},{120,... | collective-permute-start | bytes 786440 | tf_op jit(solution)/shard_map/ppermute | solution.py:460
  43.6 1.8 %collective-permute-done.below_ref = f32[16,4,8,128]{3,2,1,0:T(8,128)S(1)} collective-permute-done((f32[16,4,8,128]{3,2,1,0:T(8,128)S(1)}, f32[16,4,8,128]{3,2,1,0:T(8,128)S(1)}, u32[]{:S(2)}, u32[]{:S(2)}) %collective-permute-start) | collective-permute-done | bytes 262176 | tf_op jit(solution)/shard_map/ppermute | solution.py:460
  45.4 2.6 %collective-permute-done.1.above_ref = f32[16,4,8,128]{3,2,1,0:T(8,128)S(1)} collective-permute-done((f32[16,4,8,128]{3,2,1,0:T(8,128)S(1)}, f32[16,4,8,128]{3,2,1,0:T(8,128)S(1)}, u32[]{:S(2)}, u32[]{:S(2)}) %collective-permute-start.1) | collective-permute-done | bytes 262176 | tf_op jit(solution)/shard_map/ppermute | solution.py:460
  48.0 9.7 %shard_map.61 = (f32[16,64,128]{2,1,0:T(8,128)S(1)}, f32[4,8,128]{2,1,0:T(8,128)S(1)}) custom-call(f32[16,4,16,128]{3,2,1,0:T(8,128)S(1)} %all_to_all.20.got_ref, f32[16,4,8,128]{3,2,1,0:T(8,128)S(1)} %collective-permute-done.below_ref, f32[16,4,8,128]{3,2,1,0:T(8,128)S(1)} %collective-permute-done.1.above_ref), custom_call_target="tpu_custom_call" | custom-call | tf_op jit(solution)/shard_map/pallas_call | solution.py:468
  57.8 9.5 %all_to_all.21.table_ref = f32[4,8,128]{2,1,0:T(8,128)S(1)} all-to-all(f32[4,8,128]{2,1,0:T(8,128)S(1)} %get-tuple-element.10), channel_id=1, replica_groups={{0,128,256,384},{8,136,264,392},{16,144,272,400},{24,152,280,408},{32,1..., dimensions={0} | all-to-all | bytes 32768 | tf_op jit(solution)/shard_map/all_to_all | solution.py:500
  67.3 0.1 shard_map.62
  67.4 0.0 copy-start
  67.4 0.0 copy-start.1
  67.4 24.7 %all_to_all.22.back_ref = f32[16,72,128]{2,1,0:T(8,128)S(1)} all-to-all(f32[16,72,128]{2,1,0:T(8,128)S(1)} %shard_map.62), channel_id=1, replica_groups={{0,8,16,24,32,40,48,56,64,72,80,88,96,104,112,120},{128,136,144,152,160..., dimensions={0} | all-to-all | bytes 1179648 | tf_op jit(solution)/shard_map/all_to_all | solution.py:502
  92.1 0.0 copy-done
  92.1 0.0 copy-done.1
  92.1 0.9 shard_map.63
  93.0 17.7 %all_to_all.23 = f32[8,2,8,256]{3,2,1,0:T(8,128)S(1)} all-to-all(f32[8,2,8,256]{3,2,1,0:T(8,128)S(1)} %bitcast.12), channel_id=1, replica_groups=mesh['sub'=64,'shot'=8] {'shot'}, dimensions={0} | all-to-all | bytes 262144 | tf_op jit(solution)/shard_map/all_to_all | solution.py:506
  110.8 0.6 reduce_sum.9
  (1 shorter events, 0.0 us)
Async XLA Ops:
  37.1 8.3 %collective-permute-start = (f32[16,4,8,128]{3,2,1,0:T(8,128)S(1)}, f32[16,4,8,128]{3,2,1,0:T(8,128)S(1)}, u32[]{:S(2)}, u32[]{:S(2)}) collective-permute-start(f32[16,4,8,128]{3,2,1,0:T(8,128)S(1)} %get-tuple-element.8), channel_id=1, source_target_pairs={{8,16},{16,24},{24,32},{32,40},{40,48},{48,56},{56,0},{0,64},{64,1... | collective-permute-start | bytes 786440 | tf_op jit(solution)/shard_map/ppermute | solution.py:460
  40.1 7.9 %collective-permute-start.1 = (f32[16,4,8,128]{3,2,1,0:T(8,128)S(1)}, f32[16,4,8,128]{3,2,1,0:T(8,128)S(1)}, u32[]{:S(2)}, u32[]{:S(2)}) collective-permute-start(f32[16,4,8,128]{3,2,1,0:T(8,128)S(1)} %get-tuple-element.9), channel_id=1, source_target_pairs={{16,8},{24,16},{32,24},{40,32},{48,40},{56,48},{0,56},{64,0},{120,... | collective-permute-start | bytes 786440 | tf_op jit(solution)/shard_map/ppermute | solution.py:460
  67.4 24.7 %copy-start = (f32[1,16,8,256]{3,2,1,0:T(8,128)S(1)}, f32[1,16,8,256]{3,2,1,0:T(8,128)}, u32[]{:S(2)}) copy-start(f32[1,16,8,256]{3,2,1,0:T(8,128)} %param.7) | copy-start | bytes 393220
  67.4 24.7 %copy-start.1 = (f32[1,2,1,16,8,256]{5,4,3,2,1,0:T(8,128)S(1)}, f32[1,2,1,16,8,256]{5,4,3,2,1,0:T(8,128)}, u32[]{:S(2)}) copy-start(f32[1,2,1,16,8,256]{5,4,3,2,1,0:T(8,128)} %param.5) | copy-start | bytes 786436

commit v6 on v5

--- a/solution.py
+++ b/solution.py
@@ -29,7 +29,7 @@
 PLANES = CX + 4
 SLOT = CY + 3
 SLOTS = 6
-TILES = 9
+TILES = 8
 BASE = 8
 ROWS = BASE + TILES * TILE + 8
 BODY = slice(BASE, BASE + TILES * TILE)
@@ -279,7 +279,7 @@
     high_at = jnp.where(is_last, 30, 27)
 
     turn_ref[...] = jnp.zeros_like(turn_ref)
-    for ref in (r_ref, w_ref, d_ref, q_ref):
+    for ref in (r_ref, w_ref, q_ref):
         for plane in range(1, PLANES - 1):
             for part in range(2):
                 ref[part, plane, BODY] = jnp.zeros((TILES * TILE, LANES), jnp.float32)

time: 112 us -> 111 us (level)
  no operation moved by 1% of the time
where the time goes in v6:
time: 111 us
  blocking collectives  86.2 us (78%)
  Pallas kernels  12.6 us (11%)
  starting transfers between devices  6.49 us (6%)
  waiting for transfers between devices  4.42 us (4%)
    all_to_all x1, blocking collectives, local(): got = lax.all_to_all(message, 'sub', 0, 0, axis_index_groups=layers)  34.3 us
    all_to_all x1, blocking collectives, local(): back = lax.all_to_all(back, 'sub', 0, 0, axis_index_groups=layers)  24.7 us
    all_to_all x1, blocking collectives, local(): share = jnp.sum(lax.all_to_all(shares, 'shot', 0, 0), axis=0)  17.7 us
    pallas_call x5, Pallas kernels, run(): pl.pallas_call(kernel, out_shape=[jax.ShapeDtypeStruct(shape, jnp.float32...  12.6 us
    all_to_all x1, blocking collectives, local(): table = lax.all_to_all(sums, 'sub', 0, 0, axis_index_groups=columns)  9.53 us
    ppermute x2, starting transfers between devices, moved(): return lax.ppermute(values, ('sub', 'shot'), pairs)  6.49 us
    ppermute x2, waiting for transfers between devices, moved(): return lax.ppermute(values, ('sub', 'shot'), pairs)  4.42 us
  transfers between devices with their start and end apart: 2, of which 2 were waited for; matrix products, arithmetic and copies ran while one was open for 0% of the time, Pallas kernels for 0%

profile of v6, /device:TPU:1, one launch (start us, length us, event | category | flops | bytes accessed | tf_op | source)
XLA Modules:
  0.0 111.1 jit_solution(13083534193588794905)
XLA Ops:
  0.6 2.2 %shard_map.59 = f32[16,4,16,128]{3,2,1,0:T(8,128)} custom-call(f32[2,16,8,256]{3,2,1,0:T(8,128)} %bitcast.13, f32[16,8,256]{2,1,0:T(8,128)} %bitcast.14, f32[16,8,256]{2,1,0:T(8,128)} %bitcast.9), custom_call_target="tpu_custom_call" | custom-call | tf_op jit(solution)/shard_map/pallas_call | solution.py:468
  2.8 34.3 %all_to_all.20.got_ref = f32[16,4,16,128]{3,2,1,0:T(8,128)S(1)} all-to-all(f32[16,4,16,128]{3,2,1,0:T(8,128)} %shard_map.59), channel_id=1, replica_groups={{0,8,16,24,32,40,48,56,64,72,80,88,96,104,112,120},{128,136,144,152,160..., dimensions={0} | all-to-all | bytes 1048576 | tf_op jit(solution)/shard_map/all_to_all | solution.py:491
  37.1 3.0 %collective-permute-start = (f32[16,4,8,128]{3,2,1,0:T(8,128)S(1)}, f32[16,4,8,128]{3,2,1,0:T(8,128)S(1)}, u32[]{:S(2)}, u32[]{:S(2)}) collective-permute-start(f32[16,4,8,128]{3,2,1,0:T(8,128)S(1)} %get-tuple-element.8), channel_id=1, source_target_pairs={{8,16},{16,24},{24,32},{32,40},{40,48},{48,56},{56,0},{0,64},{64,1... | collective-permute-start | bytes 786440 | tf_op jit(solution)/shard_map/ppermute | solution.py:460
  40.1 3.5 %collective-permute-start.1 = (f32[16,4,8,128]{3,2,1,0:T(8,128)S(1)}, f32[16,4,8,128]{3,2,1,0:T(8,128)S(1)}, u32[]{:S(2)}, u32[]{:S(2)}) collective-permute-start(f32[16,4,8,128]{3,2,1,0:T(8,128)S(1)} %get-tuple-element.9), channel_id=1, source_target_pairs={{16,8},{24,16},{32,24},{40,32},{48,40},{56,48},{0,56},{64,0},{120,... | collective-permute-start | bytes 786440 | tf_op jit(solution)/shard_map/ppermute | solution.py:460
  43.6 1.8 %collective-permute-done.below_ref = f32[16,4,8,128]{3,2,1,0:T(8,128)S(1)} collective-permute-done((f32[16,4,8,128]{3,2,1,0:T(8,128)S(1)}, f32[16,4,8,128]{3,2,1,0:T(8,128)S(1)}, u32[]{:S(2)}, u32[]{:S(2)}) %collective-permute-start) | collective-permute-done | bytes 262176 | tf_op jit(solution)/shard_map/ppermute | solution.py:460
  45.4 2.6 %collective-permute-done.1.above_ref = f32[16,4,8,128]{3,2,1,0:T(8,128)S(1)} collective-permute-done((f32[16,4,8,128]{3,2,1,0:T(8,128)S(1)}, f32[16,4,8,128]{3,2,1,0:T(8,128)S(1)}, u32[]{:S(2)}, u32[]{:S(2)}) %collective-permute-start.1) | collective-permute-done | bytes 262176 | tf_op jit(solution)/shard_map/ppermute | solution.py:460
  48.0 9.4 %shard_map.61 = (f32[16,64,128]{2,1,0:T(8,128)S(1)}, f32[4,8,128]{2,1,0:T(8,128)S(1)}) custom-call(f32[16,4,16,128]{3,2,1,0:T(8,128)S(1)} %all_to_all.20.got_ref, f32[16,4,8,128]{3,2,1,0:T(8,128)S(1)} %collective-permute-done.below_ref, f32[16,4,8,128]{3,2,1,0:T(8,128)S(1)} %collective-permute-done.1.above_ref), custom_call_target="tpu_custom_call" | custom-call | tf_op jit(solution)/shard_map/pallas_call | solution.py:468
  57.4 9.5 %all_to_all.21.table_ref = f32[4,8,128]{2,1,0:T(8,128)S(1)} all-to-all(f32[4,8,128]{2,1,0:T(8,128)S(1)} %get-tuple-element.10), channel_id=1, replica_groups={{0,128,256,384},{8,136,264,392},{16,144,272,400},{24,152,280,408},{32,1..., dimensions={0} | all-to-all | bytes 32768 | tf_op jit(solution)/shard_map/all_to_all | solution.py:500
  67.0 0.1 shard_map.62
  67.0 0.0 copy-start
  67.0 0.0 copy-start.1
  67.1 24.7 %all_to_all.22.back_ref = f32[16,72,128]{2,1,0:T(8,128)S(1)} all-to-all(f32[16,72,128]{2,1,0:T(8,128)S(1)} %shard_map.62), channel_id=1, replica_groups={{0,8,16,24,32,40,48,56,64,72,80,88,96,104,112,120},{128,136,144,152,160..., dimensions={0} | all-to-all | bytes 1179648 | tf_op jit(solution)/shard_map/all_to_all | solution.py:502
  91.8 0.0 copy-done
  91.8 0.0 copy-done.1
  91.8 0.9 shard_map.63
  92.7 17.7 %all_to_all.23 = f32[8,2,8,256]{3,2,1,0:T(8,128)S(1)} all-to-all(f32[8,2,8,256]{3,2,1,0:T(8,128)S(1)} %bitcast.12), channel_id=1, replica_groups=mesh['sub'=64,'shot'=8] {'shot'}, dimensions={0} | all-to-all | bytes 262144 | tf_op jit(solution)/shard_map/all_to_all | solution.py:506
  110.4 0.6 reduce_sum.9
  (1 shorter events, 0.0 us)
Async XLA Ops:
  37.1 8.3 %collective-permute-start = (f32[16,4,8,128]{3,2,1,0:T(8,128)S(1)}, f32[16,4,8,128]{3,2,1,0:T(8,128)S(1)}, u32[]{:S(2)}, u32[]{:S(2)}) collective-permute-start(f32[16,4,8,128]{3,2,1,0:T(8,128)S(1)} %get-tuple-element.8), channel_id=1, source_target_pairs={{8,16},{16,24},{24,32},{32,40},{40,48},{48,56},{56,0},{0,64},{64,1... | collective-permute-start | bytes 786440 | tf_op jit(solution)/shard_map/ppermute | solution.py:460
  40.1 7.9 %collective-permute-start.1 = (f32[16,4,8,128]{3,2,1,0:T(8,128)S(1)}, f32[16,4,8,128]{3,2,1,0:T(8,128)S(1)}, u32[]{:S(2)}, u32[]{:S(2)}) collective-permute-start(f32[16,4,8,128]{3,2,1,0:T(8,128)S(1)} %get-tuple-element.9), channel_id=1, source_target_pairs={{16,8},{24,16},{32,24},{40,32},{48,40},{56,48},{0,56},{64,0},{120,... | collective-permute-start | bytes 786440 | tf_op jit(solution)/shard_map/ppermute | solution.py:460
  67.0 24.7 %copy-start = (f32[1,16,8,256]{3,2,1,0:T(8,128)S(1)}, f32[1,16,8,256]{3,2,1,0:T(8,128)}, u32[]{:S(2)}) copy-start(f32[1,16,8,256]{3,2,1,0:T(8,128)} %param.7) | copy-start | bytes 393220
  67.0 24.7 %copy-start.1 = (f32[1,2,1,16,8,256]{5,4,3,2,1,0:T(8,128)S(1)}, f32[1,2,1,16,8,256]{5,4,3,2,1,0:T(8,128)}, u32[]{:S(2)}) copy-start(f32[1,2,1,16,8,256]{5,4,3,2,1,0:T(8,128)} %param.5) | copy-start | bytes 786436

commit v7 on v6

--- a/solution.py
+++ b/solution.py
@@ -56,7 +56,7 @@
     return lax.broadcasted_iota(jnp.int32, values.shape, values.ndim - 1)
 
 
-def turn_kernel(source_ref, kappa_ref, damping_ref, out_ref, source_held, kappa_held, damping_held, turned_ref, sems):
+def turn_kernel(source_ref, kappa_ref, damping_ref, out_ref, source_held, kappa_held, damping_held, turned_ref, ready_ref, sems, out_sems):
     copies = [pltpu.make_async_copy(source_ref.at[0], source_held.at[0], sems.at[0]),
               pltpu.make_async_copy(source_ref.at[1], source_held.at[1], sems.at[1]),
               pltpu.make_async_copy(kappa_ref, kappa_held, sems.at[2]),
@@ -64,16 +64,20 @@
     for copy in copies:
         copy.start()
     odd, turn = path()
+    sent = []
     for field in range(FIELDS):
         copies[field].wait()
         held = (source_held.at[0], source_held.at[1], kappa_held, damping_held)[field]
         for tile in range(CZ // LANES):
             here = slice(tile * LANES, (tile + 1) * LANES)
             turned_ref[field, here] = held[:, :, here].reshape(LANES, LANES).T
-    for device in range(GROUP):
-        rows = pl.ds(pl.multiple_of(slab_of(device, odd, turn) * SLAB, SLAB), SLAB)
-        for field in range(FIELDS):
-            out_ref[device, field] = turned_ref[field, rows]
+        for device in range(GROUP):
+            rows = pl.ds(pl.multiple_of(slab_of(device, odd, turn) * SLAB, SLAB), SLAB)
+            ready_ref[field, device] = turned_ref[field, rows]
+        sent.append(pltpu.make_async_copy(ready_ref.at[field], out_ref.at[:, field], out_sems.at[field]))
+        sent[field].start()
+    for copy in sent:
+        copy.wait()
 
 
 def edges_kernel(got_ref, low_ref, high_ref):
@@ -469,7 +473,7 @@
             kernel,
             out_shape=[jax.ShapeDtypeStruct(shape, jnp.float32) for shape in out_shapes],
             in_specs=[given] * len(args),
-            out_specs=[one] * len(out_shapes),
+            out_specs=[given if space == pltpu.HBM else one] * len(out_shapes),
             scratch_shapes=list(scratch),
             compiler_params=pltpu.CompilerParams(vmem_limit_bytes=limit),
         )(*args)
@@ -483,8 +487,8 @@
     kappa = kappa[0]
     damping = damping[0]
     block = (CX, CY, CZ)
-    held = [pltpu.VMEM(shape, jnp.float32) for shape in ((2,) + block, block, block, (FIELDS, CZ, LANES))]
-    message, = call(turn_kernel, [(GROUP, FIELDS, SLAB, LANES)], held + [pltpu.SemaphoreType.DMA((FIELDS,))],
+    held = [pltpu.VMEM(shape, jnp.float32) for shape in ((2,) + block, block, block, (FIELDS, CZ, LANES), (FIELDS, GROUP, SLAB, LANES))]
+    message, = call(turn_kernel, [(GROUP, FIELDS, SLAB, LANES)], held + [pltpu.SemaphoreType.DMA((FIELDS,))] * 2,
                     pltpu.HBM, 60 * 1024 * 1024)(source, kappa, damping)
     layers = [[k * GROUP + n for n in range(GROUP)] for k in range(PZ)]
     columns = [[k * GROUP + n for k in range(PZ)] for n in range(GROUP)]

time: 111 us -> 111 us (level)
  no operation moved by 1% of the time
where the time goes in v7:
time: 111 us
  blocking collectives  86.2 us (78%)
  Pallas kernels  12.5 us (11%)
  starting transfers between devices  6.49 us (6%)
  waiting for transfers between devices  4.42 us (4%)
    all_to_all x1, blocking collectives, local(): got = lax.all_to_all(message, 'sub', 0, 0, axis_index_groups=layers)  34.3 us
    all_to_all x1, blocking collectives, local(): back = lax.all_to_all(back, 'sub', 0, 0, axis_index_groups=layers)  24.7 us
    all_to_all x1, blocking collectives, local(): share = jnp.sum(lax.all_to_all(shares, 'shot', 0, 0), axis=0)  17.7 us
    pallas_call x5, Pallas kernels, run(): pl.pallas_call(kernel, out_shape=[jax.ShapeDtypeStruct(shape, jnp.float32...  12.5 us
    all_to_all x1, blocking collectives, local(): table = lax.all_to_all(sums, 'sub', 0, 0, axis_index_groups=columns)  9.52 us
    ppermute x2, starting transfers between devices, moved(): return lax.ppermute(values, ('sub', 'shot'), pairs)  6.49 us
    ppermute x2, waiting for transfers between devices, moved(): return lax.ppermute(values, ('sub', 'shot'), pairs)  4.42 us
  transfers between devices with their start and end apart: 2, of which 2 were waited for; matrix products, arithmetic and copies ran while one was open for 0% of the time, Pallas kernels for 0%

profile of v7, /device:TPU:1, one launch (start us, length us, event | category | flops | bytes accessed | tf_op | source)
XLA Modules:
  0.0 110.9 jit_solution(4754847743827504809)
XLA Ops:
  0.6 2.1 %shard_map.59 = f32[16,4,16,128]{3,2,1,0:T(8,128)} custom-call(f32[2,16,8,256]{3,2,1,0:T(8,128)} %bitcast.13, f32[16,8,256]{2,1,0:T(8,128)} %bitcast.14, f32[16,8,256]{2,1,0:T(8,128)} %bitcast.9), custom_call_target="tpu_custom_call" | custom-call | tf_op jit(solution)/shard_map/pallas_call | solution.py:472
  2.8 34.3 %all_to_all.20.got_ref = f32[16,4,16,128]{3,2,1,0:T(8,128)S(1)} all-to-all(f32[16,4,16,128]{3,2,1,0:T(8,128)} %shard_map.59), channel_id=1, replica_groups={{0,8,16,24,32,40,48,56,64,72,80,88,96,104,112,120},{128,136,144,152,160..., dimensions={0} | all-to-all | bytes 1048576 | tf_op jit(solution)/shard_map/all_to_all | solution.py:495
  37.0 3.0 %collective-permute-start = (f32[16,4,8,128]{3,2,1,0:T(8,128)S(1)}, f32[16,4,8,128]{3,2,1,0:T(8,128)S(1)}, u32[]{:S(2)}, u32[]{:S(2)}) collective-permute-start(f32[16,4,8,128]{3,2,1,0:T(8,128)S(1)} %get-tuple-element.8), channel_id=1, source_target_pairs={{8,16},{16,24},{24,32},{32,40},{40,48},{48,56},{56,0},{0,64},{64,1... | collective-permute-start | bytes 786440 | tf_op jit(solution)/shard_map/ppermute | solution.py:464
  40.1 3.5 %collective-permute-start.1 = (f32[16,4,8,128]{3,2,1,0:T(8,128)S(1)}, f32[16,4,8,128]{3,2,1,0:T(8,128)S(1)}, u32[]{:S(2)}, u32[]{:S(2)}) collective-permute-start(f32[16,4,8,128]{3,2,1,0:T(8,128)S(1)} %get-tuple-element.9), channel_id=1, source_target_pairs={{16,8},{24,16},{32,24},{40,32},{48,40},{56,48},{0,56},{64,0},{120,... | collective-permute-start | bytes 786440 | tf_op jit(solution)/shard_map/ppermute | solution.py:464
  43.6 1.8 %collective-permute-done.below_ref = f32[16,4,8,128]{3,2,1,0:T(8,128)S(1)} collective-permute-done((f32[16,4,8,128]{3,2,1,0:T(8,128)S(1)}, f32[16,4,8,128]{3,2,1,0:T(8,128)S(1)}, u32[]{:S(2)}, u32[]{:S(2)}) %collective-permute-start) | collective-permute-done | bytes 262176 | tf_op jit(solution)/shard_map/ppermute | solution.py:464
  45.4 2.6 %collective-permute-done.1.above_ref = f32[16,4,8,128]{3,2,1,0:T(8,128)S(1)} collective-permute-done((f32[16,4,8,128]{3,2,1,0:T(8,128)S(1)}, f32[16,4,8,128]{3,2,1,0:T(8,128)S(1)}, u32[]{:S(2)}, u32[]{:S(2)}) %collective-permute-start.1) | collective-permute-done | bytes 262176 | tf_op jit(solution)/shard_map/ppermute | solution.py:464
  48.0 9.4 %shard_map.61 = (f32[16,64,128]{2,1,0:T(8,128)S(1)}, f32[4,8,128]{2,1,0:T(8,128)S(1)}) custom-call(f32[16,4,16,128]{3,2,1,0:T(8,128)S(1)} %all_to_all.20.got_ref, f32[16,4,8,128]{3,2,1,0:T(8,128)S(1)} %collective-permute-done.below_ref, f32[16,4,8,128]{3,2,1,0:T(8,128)S(1)} %collective-permute-done.1.above_ref), custom_call_target="tpu_custom_call" | custom-call | tf_op jit(solution)/shard_map/pallas_call | solution.py:472
  57.4 9.5 %all_to_all.21.table_ref = f32[4,8,128]{2,1,0:T(8,128)S(1)} all-to-all(f32[4,8,128]{2,1,0:T(8,128)S(1)} %get-tuple-element.10), channel_id=1, replica_groups={{0,128,256,384},{8,136,264,392},{16,144,272,400},{24,152,280,408},{32,1..., dimensions={0} | all-to-all | bytes 32768 | tf_op jit(solution)/shard_map/all_to_all | solution.py:504
  66.9 0.1 shard_map.62
  67.0 0.0 copy-start
  67.0 0.0 copy-start.1
  67.0 24.7 %all_to_all.22.back_ref = f32[16,72,128]{2,1,0:T(8,128)S(1)} all-to-all(f32[16,72,128]{2,1,0:T(8,128)S(1)} %shard_map.62), channel_id=1, replica_groups={{0,8,16,24,32,40,48,56,64,72,80,88,96,104,112,120},{128,136,144,152,160..., dimensions={0} | all-to-all | bytes 1179648 | tf_op jit(solution)/shard_map/all_to_all | solution.py:506
  91.7 0.0 copy-done
  91.7 0.0 copy-done.1
  91.7 0.9 shard_map.63
  92.6 17.7 %all_to_all.23 = f32[8,2,8,256]{3,2,1,0:T(8,128)S(1)} all-to-all(f32[8,2,8,256]{3,2,1,0:T(8,128)S(1)} %bitcast.12), channel_id=1, replica_groups=mesh['sub'=64,'shot'=8] {'shot'}, dimensions={0} | all-to-all | bytes 262144 | tf_op jit(solution)/shard_map/all_to_all | solution.py:510
  110.3 0.6 reduce_sum.9
  (1 shorter events, 0.0 us)
Async XLA Ops:
  37.0 8.3 %collective-permute-start = (f32[16,4,8,128]{3,2,1,0:T(8,128)S(1)}, f32[16,4,8,128]{3,2,1,0:T(8,128)S(1)}, u32[]{:S(2)}, u32[]{:S(2)}) collective-permute-start(f32[16,4,8,128]{3,2,1,0:T(8,128)S(1)} %get-tuple-element.8), channel_id=1, source_target_pairs={{8,16},{16,24},{24,32},{32,40},{40,48},{48,56},{56,0},{0,64},{64,1... | collective-permute-start | bytes 786440 | tf_op jit(solution)/shard_map/ppermute | solution.py:464
  40.1 7.9 %collective-permute-start.1 = (f32[16,4,8,128]{3,2,1,0:T(8,128)S(1)}, f32[16,4,8,128]{3,2,1,0:T(8,128)S(1)}, u32[]{:S(2)}, u32[]{:S(2)}) collective-permute-start(f32[16,4,8,128]{3,2,1,0:T(8,128)S(1)} %get-tuple-element.9), channel_id=1, source_target_pairs={{16,8},{24,16},{32,24},{40,32},{48,40},{56,48},{0,56},{64,0},{120,... | collective-permute-start | bytes 786440 | tf_op jit(solution)/shard_map/ppermute | solution.py:464
  67.0 24.8 %copy-start = (f32[1,16,8,256]{3,2,1,0:T(8,128)S(1)}, f32[1,16,8,256]{3,2,1,0:T(8,128)}, u32[]{:S(2)}) copy-start(f32[1,16,8,256]{3,2,1,0:T(8,128)} %param.7) | copy-start | bytes 393220
  67.0 24.7 %copy-start.1 = (f32[1,2,1,16,8,256]{5,4,3,2,1,0:T(8,128)S(1)}, f32[1,2,1,16,8,256]{5,4,3,2,1,0:T(8,128)}, u32[]{:S(2)}) copy-start(f32[1,2,1,16,8,256]{5,4,3,2,1,0:T(8,128)} %param.5) | copy-start | bytes 786436
